TPU v7x, 512 devices: a whole 4x8x8 slice. The times are simulated.
512 devices in a mesh: dp: 64 (over z, y), tensor: 8 (over x, core).
Axes of the slice: x: 4, y: 8, z: 8, core: 2. Of those that a mesh axis runs over, the one named last changes fastest.
Arguments:
- tokens: bfloat16 [49152, 8192], P('dp', 'tensor'), may hold values from -6 to 6
- base_value_matrix: bfloat16 [8192, 1024], P('tensor'), may hold values from -0.0625 to 0.0625
- adapter_down_factors: bfloat16 [256, 64, 8192], P('dp', None, 'tensor'), may hold values from -0.0625 to 0.0625
- adapter_up_factors: bfloat16 [256, 64, 1024], P('dp', None, 'tensor'), may hold values from -0.75 to 0.75
- adapter_storage_slot: int32 [256], replicated, may hold values from 0 to 255, as said below
- segment_adapter_ids: int32 [384], P('dp'), may hold values from 0 to 255, as said below
- segment_live_count: int32 [64], P('dp'), may hold values from 1 to 6, as said below
Outputs:
- values_out: bfloat16 [49152, 1024], P('dp', 'tensor')
Inputs may be any that keep to these rules, and one draw needn't show every extreme that they name: `adapter_storage_slot`: A permutation: every storage slot holds one adapter; slot s lies on index s // 4 of dp. `segment_adapter_ids`: every segment of index i of dp names an adapter stored on index (i + o) mod the size of dp, for some offset o with 0 <= o < 4; the first 4 segments of index i name the 4 offsets, one each, and the first segment never names offset 0; two segments of index i that name the same owner name the same adapter. `segment_live_count`: some index of dp has all 6 segments live.
All inputs are finite; a program needn't handle non-finite values.
Results may differ from a plain program's by a relative error of at most 0.0035.
Values may be sent and summed in bfloat16 or wider, within the bound.
A program may use at most 64 MiB of HBM per device.

v0:
```python
import jax
import jax.numpy as jnp
from jax import lax
from jax.sharding import PartitionSpec as P


def shifted(block, axis, distance):
    devices = range(lax.axis_size(axis))
    route = [((i - distance) % len(devices), i) for i in devices]
    return lax.ppermute(block, axis, route)


def lookup_slots(ids, adapter_storage_slot):
    table_ids = jnp.arange(adapter_storage_slot.shape[0], dtype=jnp.int32)
    matches = ids[..., None] == table_ids
    return jnp.sum(jnp.where(matches, adapter_storage_slot, 0), axis=-1)


def per_device(
    tokens,
    base_value_matrix,
    adapter_down_factors,
    adapter_up_factors,
    adapter_storage_slot,
    segment_adapter_ids,
    segment_live_count,
):
    owners_count = lax.axis_size("dp")
    my_index = lax.axis_index("dp")
    stored_adapter_count = adapter_down_factors.shape[0]
    seg_total = segment_adapter_ids.shape[0]
    seg_length = tokens.shape[0] // seg_total
    feat_share = tokens.shape[1]
    value_output_portion = adapter_up_factors.shape[2]
    rank_extent = adapter_down_factors.shape[1]
    window = min(4, seg_total)
    offset_ids = jnp.arange(window, dtype=jnp.int32)
    my_slots = lookup_slots(segment_adapter_ids, adapter_storage_slot)
    my_owner = my_slots // stored_adapter_count
    my_local = my_slots % stored_adapter_count
    my_offset = (my_owner - my_index) % owners_count
    my_live = jnp.arange(seg_total, dtype=jnp.int32) < segment_live_count[0]
    match_offset = (my_offset[:, None] == offset_ids[None, :]) & my_live[:, None]
    wanted_local = jnp.max(jnp.where(match_offset, my_local[:, None] + 1, 0), axis=0)
    asked_parts = [wanted_local[0:1]]
    for offset in range(1, window):
        asked_parts.append(shifted(wanted_local[offset : offset + 1], "dp", offset))
    asked = jnp.concatenate(asked_parts, axis=0)
    slot_chooser = (
        (asked - 1)[:, None] == jnp.arange(stored_adapter_count, dtype=jnp.int32)[None, :]
    ).astype(jnp.bfloat16)
    down_send = jnp.dot(
        slot_chooser,
        adapter_down_factors.reshape(stored_adapter_count, -1),
        preferred_element_type=jnp.float32,
    )
    down_send = down_send.astype(jnp.bfloat16).reshape(window, rank_extent, feat_share)
    up_factor_outgoing = jnp.dot(
        slot_chooser,
        adapter_up_factors.reshape(stored_adapter_count, -1),
        preferred_element_type=jnp.float32,
    )
    up_factor_outgoing = up_factor_outgoing.astype(jnp.bfloat16).reshape(
        window, rank_extent, value_output_portion
    )
    down_parts = [down_send[0]]
    up_parts = [up_factor_outgoing[0]]
    for offset in range(1, window):
        got_down, got_up = shifted((down_send[offset], up_factor_outgoing[offset]), "dp", -offset)
        down_parts.append(got_down)
        up_parts.append(got_up)
    held_down = jnp.stack(down_parts, axis=0)
    held_up = jnp.stack(up_parts, axis=0)
    selector = match_offset.astype(jnp.bfloat16)
    seg_down = jnp.dot(selector, held_down.reshape(window, -1), preferred_element_type=jnp.float32)
    seg_down = seg_down.astype(jnp.bfloat16).reshape(seg_total, rank_extent, feat_share)
    seg_up = jnp.dot(selector, held_up.reshape(window, -1), preferred_element_type=jnp.float32)
    seg_up = seg_up.astype(jnp.bfloat16).reshape(seg_total, rank_extent, value_output_portion)
    partial_value = jnp.dot(tokens, base_value_matrix, preferred_element_type=jnp.float32)
    seg_tokens = tokens.reshape(seg_total, seg_length, feat_share)
    shrink_part = jnp.einsum(
        "ksd,krd->ksr", seg_tokens, seg_down, preferred_element_type=jnp.float32
    )
    summed, down_projected = lax.psum((partial_value, shrink_part), "tensor")
    base = lax.dynamic_slice_in_dim(
        summed, lax.axis_index("tensor") * value_output_portion, value_output_portion, 1
    )
    down_projected_half = down_projected.astype(jnp.bfloat16)
    adapter_update = jnp.einsum(
        "ksr,krv->ksv", down_projected_half, seg_up, preferred_element_type=jnp.float32
    )
    adapter_update = adapter_update.reshape(tokens.shape[0], value_output_portion)
    return (base + adapter_update).astype(jnp.bfloat16)


def solution(mesh):
    placed = (
        P("dp", "tensor"),
        P("tensor", None),
        P("dp", None, "tensor"),
        P("dp", None, "tensor"),
        P(),
        P("dp"),
        P("dp"),
    )
    return jax.shard_map(
        per_device, mesh=mesh, in_specs=placed, out_specs=P("dp", "tensor"), check_vma=False
    )
```

profile of v0, /device:TPU:1, one launch (start us, length us, event | category | flops | bytes accessed | tf_op | source)
XLA Modules:
  0.0 118.3 jit_solution(4660016104779050277)
XLA Ops:
  6.5 0.0 copy-start
  6.5 0.0 all-reduce.3.cloned.1.call-start
  7.4 0.9 select_reduce_fusion
  8.2 0.1 select_reduce_fusion.1
  8.4 0.7 fusion.33
  9.0 6.0 %collective-permute-start.2 = (s32[1]{0:T(128)}, s32[1]{0:T(128)}, u32[]{:S(2)}, u32[]{:S(2)}) collective-permute-start(s32[1]{0:T(128)} %get-tuple-element.14), channel_id=1, source_target_pairs={{488,0},{496,8},{504,16},{0,24},{8,32},{16,40},{24,48},{32,56},{40... | collective-permute-start | bytes 20 | tf_op jit(solution)/shard_map/ppermute | solution.py:10
  15.1 4.5 %collective-permute-start.1 = (s32[1]{0:T(128)}, s32[1]{0:T(128)}, u32[]{:S(2)}, u32[]{:S(2)}) collective-permute-start(s32[1]{0:T(128)} %get-tuple-element.15), channel_id=1, source_target_pairs={{496,0},{504,8},{0,16},{8,24},{16,32},{24,40},{32,48},{40,56},{48,... | collective-permute-start | bytes 20 | tf_op jit(solution)/shard_map/ppermute | solution.py:10
  19.6 2.3 %collective-permute-start = (s32[1]{0:T(128)}, s32[1]{0:T(128)}, u32[]{:S(2)}, u32[]{:S(2)}) collective-permute-start(s32[1]{0:T(128)} %get-tuple-element.16), channel_id=1, source_target_pairs={{504,0},{0,8},{8,16},{16,24},{24,32},{32,40},{40,48},{48,56},{56,6... | collective-permute-start | bytes 20 | tf_op jit(solution)/shard_map/ppermute | solution.py:10
  21.9 0.0 copy-done
  21.9 4.9 %fusion.34 = f32[768,1024]{1,0:T(8,128)} fusion(bf16[768,1024]{1,0:T(8,128)(2,1)} %param.7, bf16[1024,1024]{1,0:T(8,128)(2,1)S(1)} %copy-done), kind=kOutput, calls=%fused_computation.62 | convolution fusion | flops 1610612736 | bytes 6815744 | tf_op jit(solution)/shard_map/dot_general | solution.py:79
  26.8 0.0 copy-start.2
  26.8 0.0 copy-start.3
  26.8 0.0 all-reduce.3.cloned.1.call-update
  26.9 1.0 copy-done.2
  27.9 0.4 copy.8
  28.3 0.0 collective-permute-done.2
  28.3 0.0 collective-permute-done.1
  28.3 0.2 collective-permute-done
  28.5 2.6 %add_add_fusion = s32[4]{0:T(128)S(1)} fusion(s32[1]{0:T(128)} %collective-permute-done.2, s32[1]{0:T(128)} %collective-permute-done.1, s32[1]{0:T(128)} %collective-permute-done, s32[1]{0:T(128)} %get-tuple-element.13), kind=kLoop, calls=%fused_computation.57 | loop fusion | flops 16 | bytes 32 | tf_op jit(solution)/shard_map/sub | solution.py:50
  31.1 0.0 copy-done.3
  31.1 0.2 convolution_convert_fusion.3
  31.4 0.3 slice_reduce_fusion.5
  31.6 9.2 %collective-permute-start.8 = (bf16[64,128]{1,0:T(8,128)(2,1)S(1)}, bf16[64,128]{1,0:T(8,128)(2,1)S(1)}, u32[]{:S(2)}, u32[]{:S(2)}) collective-permute-start(bf16[64,128]{1,0:T(8,128)(2,1)S(1)} %bitcast.74), channel_id=1, source_target_pairs={{24,0},{32,8},{40,16},{48,24},{56,32},{64,40},{72,48},{80,56},{88,... | collective-permute-start | bytes 49160 | tf_op jit(solution)/shard_map/ppermute | solution.py:10
  40.8 3.4 %collective-permute-start.6 = (bf16[64,128]{1,0:T(8,128)(2,1)S(1)}, bf16[64,128]{1,0:T(8,128)(2,1)S(1)}, u32[]{:S(2)}, u32[]{:S(2)}) collective-permute-start(bf16[64,128]{1,0:T(8,128)(2,1)S(1)} %bitcast.73), channel_id=1, source_target_pairs={{8,0},{16,8},{24,16},{32,24},{40,32},{48,40},{56,48},{64,56},{72,6... | collective-permute-start | bytes 49160 | tf_op jit(solution)/shard_map/ppermute | solution.py:10
  44.2 5.2 %collective-permute-start.7 = (bf16[64,128]{1,0:T(8,128)(2,1)S(1)}, bf16[64,128]{1,0:T(8,128)(2,1)S(1)}, u32[]{:S(2)}, u32[]{:S(2)}) collective-permute-start(bf16[64,128]{1,0:T(8,128)(2,1)S(1)} %bitcast.72), channel_id=1, source_target_pairs={{16,0},{24,8},{32,16},{40,24},{48,32},{56,40},{64,48},{72,56},{80,... | collective-permute-start | bytes 49160 | tf_op jit(solution)/shard_map/ppermute | solution.py:10
  49.4 0.5 convolution_convert_fusion.1
  49.9 2.4 %slice_reduce_fusion.2 = (bf16[65536]{0:T(1024)(128)(2,1)S(1)}, bf16[65536]{0:T(1024)(128)(2,1)S(1)}, bf16[65536]{0:T(1024)(128)(2,1)S(1)}, bf16[1,65536]{1,0:T(2,128)(2,1)S(1)}) fusion(bf16[4,65536]{1,0:T(4,128)(2,1)S(1)} %convolution_convert_fusion.1), kind=kLoop, calls=%fused_computation.19 | loop fusion | bytes 1048576 | tf_op jit(solution)/shard_map/slice | solution.py:69
  52.3 0.1 squeeze.23
  52.3 4.1 %collective-permute-start.4 = (bf16[64,1024]{1,0:T(8,128)(2,1)S(1)}, bf16[64,1024]{1,0:T(8,128)(2,1)S(1)}, u32[]{:S(2)}, u32[]{:S(2)}) collective-permute-start(bf16[64,1024]{1,0:T(8,128)(2,1)S(1)} %squeeze.23), channel_id=1, source_target_pairs={{16,0},{24,8},{32,16},{40,24},{48,32},{56,40},{64,48},{72,56},{80,... | collective-permute-start | bytes 393224 | tf_op jit(solution)/shard_map/ppermute | solution.py:10
  56.5 0.1 squeeze.24
  56.6 5.6 %collective-permute-start.5 = (bf16[64,1024]{1,0:T(8,128)(2,1)S(1)}, bf16[64,1024]{1,0:T(8,128)(2,1)S(1)}, u32[]{:S(2)}, u32[]{:S(2)}) collective-permute-start(bf16[64,1024]{1,0:T(8,128)(2,1)S(1)} %squeeze.24), channel_id=1, source_target_pairs={{24,0},{32,8},{40,16},{48,24},{56,32},{64,40},{72,48},{80,56},{88,... | collective-permute-start | bytes 393224 | tf_op jit(solution)/shard_map/ppermute | solution.py:10
  62.2 0.1 squeeze.22
  62.2 0.0 collective-permute-done.8
  62.2 2.2 %collective-permute-start.3 = (bf16[64,1024]{1,0:T(8,128)(2,1)S(1)}, bf16[64,1024]{1,0:T(8,128)(2,1)S(1)}, u32[]{:S(2)}, u32[]{:S(2)}) collective-permute-start(bf16[64,1024]{1,0:T(8,128)(2,1)S(1)} %squeeze.22), channel_id=1, source_target_pairs={{8,0},{16,8},{24,16},{32,24},{40,32},{48,40},{56,48},{64,56},{72,6... | collective-permute-start | bytes 393224 | tf_op jit(solution)/shard_map/ppermute | solution.py:10
  64.5 0.0 collective-permute-done.6
  64.5 0.0 collective-permute-done.7
  64.6 0.3 fusion
  64.9 0.0 collective-permute-done.4
  64.9 0.2 copy.10
  65.1 0.4 collective-permute-done.5
  65.5 0.2 copy.11
  65.7 0.0 copy-start.1
  65.8 8.8 %collective-permute-done.3 = bf16[64,1024]{1,0:T(8,128)(2,1)S(1)} collective-permute-done((bf16[64,1024]{1,0:T(8,128)(2,1)S(1)}, bf16[64,1024]{1,0:T(8,128)(2,1)S(1)}, u32[]{:S(2)}, u32[]{:S(2)}) %collective-permute-start.3) | collective-permute-done | bytes 131104 | tf_op jit(solution)/shard_map/ppermute | solution.py:10
  74.5 0.2 copy.9
  74.8 1.4 %convolution_convert_fusion = bf16[6,65536]{1,0:T(8,128)(2,1)S(1)} fusion(bf16[1,65536]{1,0:T(2,128)(2,1)S(1)} %bitcast.61, bf16[1,65536]{1,0:T(2,128)(2,1)S(1)} %bitcast.60, bf16[1,65536]{1,0:T(2,128)(2,1)S(1)} %bitcast.62, bf16[1,65536]{1,0:T(2,128)(2,1)S(1)} %get-tuple-element.11, s32[6]{0:T(128)S(1)} %get-tuple-element.17, ...), kind=kOutput, calls=%fused_computation | convolution fusion | flops 5636144 | bytes 1310750 | tf_op jit(solution)/shard_map/dot_general | solution.py:75
  76.2 0.0 copy-done.1
  76.2 0.7 convolution_bitcast_fusion
  76.9 25.0 %all-reduce.4 = bf16[6,128,64]{1,2,0:T(8,128)(2,1)S(1)} all-reduce(f32[6,128,64]{1,2,0:T(8,128)S(1)} %convolution_bitcast_fusion), channel_id=1, replica_groups=mesh['dp'=64,'tensor'=8] {'tensor'}, use_global_device_ids=true, to_apply=%region_3.4 | all-reduce | flops 49152 | bytes 294912 | tf_op jit(solution)/shard_map/psum | solution.py:84
  102.0 0.3 fusion.11
  102.3 7.5 %all-reduce.3.cloned.1.call-done = f32[768,1024]{1,0:T(8,128)} async-done(((f32[768,1024]{1,0:T(8,128)}), f32[768,1024]{1,0:T(8,128)}) %all-reduce.3.cloned.1.call-update) | async-done | bytes 3145744 | tf_op jit(solution)/shard_map/psum | solution.py:84
  109.8 1.7 %fusion.10 = bf16[768,128]{1,0:T(8,128)(2,1)} fusion(f32[6,128,128]{2,1,0:T(8,128)S(1)} %fusion.11, f32[768,1024]{1,0:T(8,128)} %all-reduce.3.cloned.1.call-done, s32[]{:T(128)S(6)} %select_n.39), kind=kLoop, calls=%fused_computation.16 | loop fusion | flops 196608 | bytes 983044 | tf_op jit(solution)/shard_map/convert_element_type | solution.py:93
  (5 shorter events, 0.1 us)
Async XLA Ops:
  6.5 15.4 %copy-start = (bf16[1024,1024]{1,0:T(8,128)(2,1)S(1)}, bf16[1024,1024]{1,0:T(8,128)(2,1)}, u32[]{:S(2)}) copy-start(bf16[1024,1024]{1,0:T(8,128)(2,1)} %param.8) | copy-start | bytes 6291460
  6.5 103.2 %all-reduce.3.cloned.1.call-start = ((), (), s32[]{:S(2)}) async-start(), calls=%async_computation | async-start | bytes 6291456 | tf_op jit(solution)/shard_map/psum | solution.py:84
  9.0 19.3 %collective-permute-start.2 = (s32[1]{0:T(128)}, s32[1]{0:T(128)}, u32[]{:S(2)}, u32[]{:S(2)}) collective-permute-start(s32[1]{0:T(128)} %get-tuple-element.14), channel_id=1, source_target_pairs={{488,0},{496,8},{504,16},{0,24},{8,32},{16,40},{24,48},{32,56},{40... | collective-permute-start | bytes 20 | tf_op jit(solution)/shard_map/ppermute | solution.py:10
  15.1 13.2 %collective-permute-start.1 = (s32[1]{0:T(128)}, s32[1]{0:T(128)}, u32[]{:S(2)}, u32[]{:S(2)}) collective-permute-start(s32[1]{0:T(128)} %get-tuple-element.15), channel_id=1, source_target_pairs={{496,0},{504,8},{0,16},{8,24},{16,32},{24,40},{32,48},{40,56},{48,... | collective-permute-start | bytes 20 | tf_op jit(solution)/shard_map/ppermute | solution.py:10
  19.6 8.9 %collective-permute-start = (s32[1]{0:T(128)}, s32[1]{0:T(128)}, u32[]{:S(2)}, u32[]{:S(2)}) collective-permute-start(s32[1]{0:T(128)} %get-tuple-element.16), channel_id=1, source_target_pairs={{504,0},{0,8},{8,16},{16,24},{24,32},{32,40},{40,48},{48,56},{56,6... | collective-permute-start | bytes 20 | tf_op jit(solution)/shard_map/ppermute | solution.py:10
  26.8 1.0 copy-start.2
  26.8 4.3 %copy-start.3 = (bf16[4,64,128]{2,1,0:T(8,128)(2,1)S(1)}, bf16[4,64,128]{2,1,0:T(8,128)(2,1)}, u32[]{:S(2)}) copy-start(bf16[4,64,128]{2,1,0:T(8,128)(2,1)} %param.10) | copy-start | bytes 196612
  31.6 30.6 %collective-permute-start.8 = (bf16[64,128]{1,0:T(8,128)(2,1)S(1)}, bf16[64,128]{1,0:T(8,128)(2,1)S(1)}, u32[]{:S(2)}, u32[]{:S(2)}) collective-permute-start(bf16[64,128]{1,0:T(8,128)(2,1)S(1)} %bitcast.74), channel_id=1, source_target_pairs={{24,0},{32,8},{40,16},{48,24},{56,32},{64,40},{72,48},{80,56},{88,... | collective-permute-start | bytes 49160 | tf_op jit(solution)/shard_map/ppermute | solution.py:10
  40.8 23.7 %collective-permute-start.6 = (bf16[64,128]{1,0:T(8,128)(2,1)S(1)}, bf16[64,128]{1,0:T(8,128)(2,1)S(1)}, u32[]{:S(2)}, u32[]{:S(2)}) collective-permute-start(bf16[64,128]{1,0:T(8,128)(2,1)S(1)} %bitcast.73), channel_id=1, source_target_pairs={{8,0},{16,8},{24,16},{32,24},{40,32},{48,40},{56,48},{64,56},{72,6... | collective-permute-start | bytes 49160 | tf_op jit(solution)/shard_map/ppermute | solution.py:10
  44.2 20.3 %collective-permute-start.7 = (bf16[64,128]{1,0:T(8,128)(2,1)S(1)}, bf16[64,128]{1,0:T(8,128)(2,1)S(1)}, u32[]{:S(2)}, u32[]{:S(2)}) collective-permute-start(bf16[64,128]{1,0:T(8,128)(2,1)S(1)} %bitcast.72), channel_id=1, source_target_pairs={{16,0},{24,8},{32,16},{40,24},{48,32},{56,40},{64,48},{72,56},{80,... | collective-permute-start | bytes 49160 | tf_op jit(solution)/shard_map/ppermute | solution.py:10
  52.3 12.5 %collective-permute-start.4 = (bf16[64,1024]{1,0:T(8,128)(2,1)S(1)}, bf16[64,1024]{1,0:T(8,128)(2,1)S(1)}, u32[]{:S(2)}, u32[]{:S(2)}) collective-permute-start(bf16[64,1024]{1,0:T(8,128)(2,1)S(1)} %squeeze.23), channel_id=1, source_target_pairs={{16,0},{24,8},{32,16},{40,24},{48,32},{56,40},{64,48},{72,56},{80,... | collective-permute-start | bytes 393224 | tf_op jit(solution)/shard_map/ppermute | solution.py:10
  56.6 9.0 %collective-permute-start.5 = (bf16[64,1024]{1,0:T(8,128)(2,1)S(1)}, bf16[64,1024]{1,0:T(8,128)(2,1)S(1)}, u32[]{:S(2)}, u32[]{:S(2)}) collective-permute-start(bf16[64,1024]{1,0:T(8,128)(2,1)S(1)} %squeeze.24), channel_id=1, source_target_pairs={{24,0},{32,8},{40,16},{48,24},{56,32},{64,40},{72,48},{80,56},{88,... | collective-permute-start | bytes 393224 | tf_op jit(solution)/shard_map/ppermute | solution.py:10
  62.2 12.3 %collective-permute-start.3 = (bf16[64,1024]{1,0:T(8,128)(2,1)S(1)}, bf16[64,1024]{1,0:T(8,128)(2,1)S(1)}, u32[]{:S(2)}, u32[]{:S(2)}) collective-permute-start(bf16[64,1024]{1,0:T(8,128)(2,1)S(1)} %squeeze.22), channel_id=1, source_target_pairs={{8,0},{16,8},{24,16},{32,24},{40,32},{48,40},{56,48},{64,56},{72,6... | collective-permute-start | bytes 393224 | tf_op jit(solution)/shard_map/ppermute | solution.py:10
  65.7 10.5 %copy-start.1 = (bf16[768,1024]{1,0:T(8,128)(2,1)S(1)}, bf16[768,1024]{1,0:T(8,128)(2,1)}, u32[]{:S(2)}) copy-start(bf16[768,1024]{1,0:T(8,128)(2,1)} %param.7) | copy-start | bytes 4718596
Sparse Core Ops, SparseCore 0:
  27.0 82.7 all-reduce.2
where the time goes:
time: 119 us; the launch traced here: 118 us
  starting transfers between devices  42.5 us (36%)
  blocking collectives  25 us (21%)
  waiting for transfers between devices  17 us (14%)
  between operations  14.5 us (12%)
  matrix products  8.33 us (7%)
  local copies, waits for them, and re-layouts  5.62 us (5%)
  other arithmetic  5.36 us (5%)
    ppermute x9, starting transfers between devices, shifted(): return lax.ppermute(block, axis, route)  42.5 us
    psum x1, blocking collectives, per_device(): summed, down_projected = lax.psum((partial_value, shrink_part), 'tensor')  25 us
    ppermute x9, waiting for transfers between devices, shifted(): return lax.ppermute(block, axis, route)  9.45 us
    psum x1, waiting for transfers between devices, per_device(): summed, down_projected = lax.psum((partial_value, shrink_part), 'tensor')  7.51 us
    dot_general x1, matrix products, per_device(): jnp.dot(tokens, base_value_matrix, preferred_element_type=jnp.float32)  4.9 us
    sub x1, other arithmetic, per_device(): asked - 1  2.61 us
  transfers between devices with their start and end apart: 10, of which 4 were waited for; matrix products, arithmetic and copies ran while one was open for 13% of the time, Pallas kernels for 0%

commit v1 on v0

v1 whole, which is shorter than its diff:
```python
import functools

import jax
import jax.numpy as jnp
from jax import lax
from jax.experimental import pallas as pl
from jax.experimental.pallas import tpu as pltpu
from jax.sharding import PartitionSpec as P

MESH = pl.DeviceIdType.MESH
F32 = jnp.float32
BF16 = jnp.bfloat16

RING = 8
SEG = 128
RANK = 64
DIRECT = 32
PIECE = 16
PIECES = (RANK - DIRECT) // PIECE
ORDER = (2, 1, 3, 0)


def nt_dot(a, b):
    return lax.dot_general(a, b, (((1,), (1,)), ((), ())), preferred_element_type=F32)


def twice(a):
    return jnp.concatenate([a, a], axis=0)


def kernel(
    n_dp,
    n_tensor,
    tokens_hbm,
    w_hbm,
    down_hbm,
    up_hbm,
    slot_hbm,
    ids_hbm,
    live_hbm,
    out_ref,
    tok,
    w,
    down,
    up,
    slot,
    ids,
    live,
    req_out,
    req_in,
    a_out,
    a_near,
    a_far,
    relay,
    b_out,
    b_near,
    b_far,
    mine,
    core_out,
    core_in,
    x_out,
    x_in,
    s_mine,
    s_out,
    s_in,
    t_mine,
    t_out,
    t_in,
    acc,
    load_sem,
    req_send,
    req_recv,
    a_send,
    a_recv,
    relay_send,
    relay_recv,
    pass_send,
    pass_recv,
    b_send,
    b_recv,
    core_send,
    core_recv,
    x_send,
    x_recv,
    s_send,
    s_recv,
    t_send,
    t_recv,
):
    me = lax.axis_index("dp")
    t = lax.axis_index("tensor")
    n_chip = n_tensor // 2
    segs = tok.shape[0]
    stored = down.shape[0]

    def dp_at(offset):
        return (lax.rem(me + offset + n_dp, n_dp), t)

    def tensor_at(offset):
        return (me, lax.rem(t + offset, n_tensor))

    other_core = (me, t + 1 - 2 * lax.rem(t, 2))
    row = me // RING * RING
    y = lax.rem(me, RING)
    relay_to = (row + lax.rem(y + 2, RING), t)
    relay_from = (row + lax.rem(y + RING - 2, RING), t)
    pass_to = (lax.rem(row + lax.rem(y + RING - 2, RING) - 3 + n_dp, n_dp), t)
    far_owner = lax.rem(me + 3, n_dp)
    pass_from = (far_owner // RING * RING + lax.rem(lax.rem(far_owner, RING) + 2, RING), t)

    def remote(src, dst, send, recv, device):
        return pltpu.make_async_remote_copy(
            src_ref=src, dst_ref=dst, send_sem=send, recv_sem=recv, device_id=device, device_id_type=MESH
        )

    barrier = pltpu.get_barrier_semaphore()
    peers = [dp_at(o) for o in (1, 2, 3, -1, -2, -3)]
    peers += [relay_to, relay_from, pass_to, pass_from]
    peers += [tensor_at(k) for k in range(1, n_tensor)]
    for peer in peers:
        pl.semaphore_signal(barrier, inc=1, device_id=peer, device_id_type=MESH)

    small = [
        pltpu.make_async_copy(src, dst, load_sem.at[i])
        for i, (src, dst) in enumerate(((slot_hbm, slot), (ids_hbm, ids), (live_hbm, live)))
    ]
    down_load = pltpu.make_async_copy(down_hbm, down, load_sem.at[3])
    up_load = pltpu.make_async_copy(up_hbm, up, load_sem.at[4])
    tok_load = pltpu.make_async_copy(tokens_hbm, tok, load_sem.at[5])
    w_load = []
    for i, k in enumerate(ORDER):
        for half in range(2):
            owner = lax.rem(t + 2 * k, n_tensor)
            if half:
                owner = owner + 1 - 2 * lax.rem(owner, 2)
            columns = pl.ds(pl.multiple_of(owner * 128, 128), 128)
            w_load.append(
                pltpu.make_async_copy(
                    w_hbm.at[:, columns], w.at[i, :, pl.ds(half * 128, 128)], load_sem.at[6 + 2 * i + half]
                )
            )
    for copy in small:
        copy.start()
    down_load.start()
    tok_load.start()
    for copy in w_load:
        copy.start()
    up_load.start()

    for copy in small:
        copy.wait()
    offs, locs = [], []
    for s in range(segs):
        place = slot[ids[s]]
        offs.append(lax.rem(place // stored - me + n_dp, n_dp))
        locs.append(lax.rem(place, stored))
    wanted = []
    for o in range(4):
        found = jnp.int32(0)
        for s in range(4):
            found = jnp.where(offs[s] == o, locs[s], found)
        wanted.append(found)
    far_seg = jnp.int32(0)
    for s in range(4):
        far_seg = jnp.where(offs[s] == 3, s, far_seg)
    live_count = live[0]
    for o in range(1, 4):
        req_out[o - 1] = jnp.full(req_out.shape[1:], wanted[o], jnp.int32)

    pl.semaphore_wait(barrier, len(peers))
    asks = [
        remote(req_out.at[o - 1], req_in.at[o - 1], req_send.at[o - 1], req_recv.at[o - 1], dp_at(o))
        for o in range(1, 4)
    ]
    for copy in asks:
        copy.start()

    core_copies = []

    def base_block(i):
        w_load[2 * i].wait()
        w_load[2 * i + 1].wait()

        def rows(s, carry):
            part = jnp.dot(tok[s], w[i], preferred_element_type=F32)
            mine[i, s] = part[:, :128]
            core_out[i, s] = part[:, 128:]
            return carry

        lax.fori_loop(0, segs, rows, 0)
        copy = remote(core_out.at[i], core_in.at[i], core_send.at[i], core_recv.at[i], other_core)
        copy.start()
        core_copies.append(copy)

    a_copies, relay_copies, b_copies = [], [], []

    def serve(o):
        asks[o - 1].wait_recv()
        pick = jnp.max(req_in[o - 1])
        a_out[o - 1] = down[pick]
        b_out[o - 1] = up[pick]
        dst = a_near.at[o] if o < 3 else a_far
        rows = RANK if o < 3 else DIRECT
        copy = remote(
            a_out.at[o - 1, pl.ds(0, rows)], dst.at[pl.ds(0, rows)], a_send.at[o - 1], a_recv.at[o - 1], dp_at(-o)
        )
        copy.start()
        a_copies.append(copy)
        if o == 3:
            for j in range(PIECES):
                copy = remote(
                    a_out.at[o - 1, pl.ds(DIRECT + j * PIECE, PIECE)],
                    relay.at[j],
                    relay_send.at[j],
                    relay_recv.at[j],
                    relay_to,
                )
                copy.start()
                relay_copies.append(copy)

    tok_load.wait()
    base_block(0)
    down_load.wait()
    up_load.wait()
    a_near[0] = down[wanted[0]]
    b_near[0] = twice(up[wanted[0]])
    base_block(1)
    serve(1)
    base_block(2)
    serve(2)
    serve(3)
    base_block(3)

    x_copies = []
    for i in range(3):
        core_copies[i].wait_recv()
        x_out[i] = (mine[i] + core_in[i]).astype(BF16)
        copy = remote(x_out.at[i], x_in.at[i], x_send.at[i], x_recv.at[i], tensor_at(2 * ORDER[i]))
        copy.start()
        x_copies.append(copy)

    pass_copies = []
    for j in range(PIECES):
        relay_copies[j].wait_recv()
        copy = remote(
            relay.at[j], a_far.at[pl.ds(DIRECT + j * PIECE, PIECE)], pass_send.at[j], pass_recv.at[j], pass_to
        )
        copy.start()
        pass_copies.append(copy)

    for o in range(1, 4):
        dst = b_near.at[o, pl.ds(0, RANK)] if o < 3 else b_far
        copy = remote(b_out.at[o - 1], dst, b_send.at[o - 1], b_recv.at[o - 1], dp_at(-o))
        copy.start()
        b_copies.append(copy)

    low_lanes = lax.broadcasted_iota(jnp.int32, (SEG, 128), 1) < RANK
    half = segs // 2

    a_copies[0].wait_recv()
    a_copies[1].wait_recv()

    def near_shrink(s):
        return nt_dot(tok[s], twice(a_near[jnp.minimum(offs[s], 2)]))

    for j in range(half):
        packed = jnp.where(low_lanes, near_shrink(j), near_shrink(j + half))
        s_mine[j] = packed
        s_out[j] = packed.astype(BF16)
    s_copies = []
    for k in range(1, n_tensor):
        copy = remote(s_out, s_in.at[k - 1], s_send.at[k - 1], s_recv.at[k - 1], tensor_at(k))
        copy.start()
        s_copies.append(copy)

    a_copies[2].wait_recv()
    for copy in pass_copies:
        copy.wait_recv()
    far = twice(a_far[...])
    first = nt_dot(tok[far_seg], far)
    second = nt_dot(tok[segs - 2], far)
    third = nt_dot(tok[segs - 1], far)
    h = SEG // 2
    packed = jnp.concatenate(
        [jnp.where(low_lanes, first, second), jnp.where(low_lanes[:h], third[:h], third[h:])], axis=0
    )
    t_mine[...] = packed
    t_out[...] = packed.astype(BF16)
    t_copies = []
    for k in range(1, n_tensor):
        copy = remote(t_out, t_in.at[k - 1], t_send.at[k - 1], t_recv.at[k - 1], tensor_at(k))
        copy.start()
        t_copies.append(copy)

    core_copies[3].wait_recv()
    for copy in x_copies:
        copy.wait_recv()
    acc[...] = (
        mine[3] + core_in[3] + x_in[0].astype(F32) + x_in[1].astype(F32) + x_in[2].astype(F32)
    )

    b_copies[0].wait_recv()
    b_copies[1].wait_recv()
    for o in (1, 2):
        b_near[o, RANK:] = b_near[o, :RANK]
    for copy in s_copies:
        copy.wait_recv()
    for j in range(half):
        total = s_mine[j]
        for k in range(n_tensor - 1):
            total = total + s_in[k, j].astype(F32)
        for s, keep in ((j, low_lanes), (j + half, ~low_lanes)):
            x = jnp.where(keep, total, 0.0).astype(BF16)
            add = jnp.dot(x, b_near[jnp.minimum(offs[s], 2)], preferred_element_type=F32)
            used = (offs[s] < 3) & (s < live_count)
            acc[s] += jnp.where(used, add, 0.0)

    b_copies[2].wait_recv()
    bf = twice(b_far[...])
    for copy in t_copies:
        copy.wait_recv()
    total = t_mine[...]
    for k in range(n_tensor - 1):
        total = total + t_in[k].astype(F32)
    top, low = total[:SEG], total[SEG:]

    def far_delta(x, keep):
        return jnp.dot(jnp.where(keep, x, 0.0).astype(BF16), bf, preferred_element_type=F32)

    first = far_delta(top, low_lanes)
    second = far_delta(top, ~low_lanes)
    third = jnp.concatenate([far_delta(low, low_lanes[:h]), far_delta(low, ~low_lanes[:h])], axis=0)
    for s in range(segs):
        add = first if s < 4 else second if s == segs - 2 else third
        used = (offs[s] == 3) & (s < live_count)
        out_ref[pl.ds(s * SEG, SEG), :] = (acc[s] + jnp.where(used, add, 0.0)).astype(out_ref.dtype)

    for copy in asks + a_copies + relay_copies + pass_copies + b_copies + core_copies + x_copies + s_copies + t_copies:
        copy.wait_send()


def per_device(n_dp, n_tensor, tokens, w, down, up, slot, ids, live):
    rows, width = tokens.shape
    segs = ids.shape[0]
    stored, rank, columns = up.shape
    peers = n_tensor - 1
    dma = pltpu.SemaphoreType.DMA
    vmem, smem = pltpu.VMEM, pltpu.SMEM
    return pl.pallas_call(
        functools.partial(kernel, n_dp, n_tensor),
        name="adapted_projection",
        out_shape=jax.ShapeDtypeStruct((rows, columns), BF16),
        in_specs=[pl.BlockSpec(memory_space=pl.ANY)] * 7,
        out_specs=pl.BlockSpec(memory_space=pltpu.VMEM),
        scratch_shapes=[
            vmem((segs, SEG, width), BF16),
            vmem((4, width, 2 * columns), BF16),
            vmem((stored, rank, width), BF16),
            vmem((stored, rank, columns), BF16),
            smem(slot.shape, jnp.int32),
            smem(ids.shape, jnp.int32),
            smem(live.shape, jnp.int32),
            vmem((3, 8, 128), jnp.int32),
            vmem((3, 8, 128), jnp.int32),
            vmem((3, rank, width), BF16),
            vmem((3, rank, width), BF16),
            vmem((rank, width), BF16),
            vmem((PIECES, PIECE, width), BF16),
            vmem((3, rank, columns), BF16),
            vmem((3, 2 * rank, columns), BF16),
            vmem((rank, columns), BF16),
            vmem((4, segs, SEG, columns), F32),
            vmem((4, segs, SEG, columns), F32),
            vmem((4, segs, SEG, columns), F32),
            vmem((3, segs, SEG, columns), BF16),
            vmem((3, segs, SEG, columns), BF16),
            vmem((segs // 2, SEG, 128), F32),
            vmem((segs // 2, SEG, 128), BF16),
            vmem((peers, segs // 2, SEG, 128), BF16),
            vmem((SEG + SEG // 2, 128), F32),
            vmem((SEG + SEG // 2, 128), BF16),
            vmem((peers, SEG + SEG // 2, 128), BF16),
            vmem((segs, SEG, columns), F32),
            dma((14,)),
            dma((3,)),
            dma((3,)),
            dma((3,)),
            dma((3,)),
            dma((PIECES,)),
            dma((PIECES,)),
            dma((PIECES,)),
            dma((PIECES,)),
            dma((3,)),
            dma((3,)),
            dma((4,)),
            dma((4,)),
            dma((3,)),
            dma((3,)),
            dma((peers,)),
            dma((peers,)),
            dma((peers,)),
            dma((peers,)),
        ],
        compiler_params=pltpu.CompilerParams(
            collective_id=0, has_side_effects=True, vmem_limit_bytes=63 * 1024 * 1024
        ),
        cost_estimate=pl.CostEstimate(flops=2_000_000_000, bytes_accessed=4_500_000, transcendentals=0),
    )(tokens.reshape(segs, SEG, width), w, down, up, slot, ids, live)


def solution(mesh):
    placed = (
        P("dp", "tensor"),
        P("tensor", None),
        P("dp", None, "tensor"),
        P("dp", None, "tensor"),
        P(),
        P("dp"),
        P("dp"),
    )
    return jax.shard_map(
        functools.partial(per_device, mesh.shape["dp"], mesh.shape["tensor"]),
        mesh=mesh,
        in_specs=placed,
        out_specs=P("dp", "tensor"),
        check_vma=False,
    )
```

time: 119 us -> 50.1 us (0.42)
  Pallas kernels: 0 us -> 47.7 us
  starting transfers between devices: 42.5 us -> 0 us
  blocking collectives: 25 us -> 0 us
  waiting for transfers between devices: 17 us -> 0 us
  between operations: 14.5 us -> 0.66 us
  matrix products: 8.33 us -> 0 us
  other arithmetic: 5.36 us -> 0 us
  local copies, waits for them, and re-layouts: 5.62 us -> 1.62 us
    pallas_call x0 -> x1, Pallas kernels: none -> 47.7 us  [per_device(): pl.pallas_call(functools.partial(kernel, n_dp, n_tensor), name='adapted_p...]
    ppermute x9 -> x0, starting transfers between devices: 42.5 us -> none  [shifted(): return lax.ppermute(block, axis, route)]
    psum x1 -> x0, blocking collectives: 25 us -> none  [per_device(): summed, down_projected = lax.psum((partial_value, shrink_part), 'tensor')]
    ppermute x9 -> x0, waiting for transfers between devices: 9.45 us -> none  [shifted(): return lax.ppermute(block, axis, route)]
    dot_general x7 -> x0, matrix products: 8.33 us -> none  [the longest x1 4.9 us: per_device(): jnp.dot(tokens, base_value_matrix, preferred_element_type=jnp.float32)]
    psum x1 -> x0, waiting for transfers between devices: 7.51 us -> none  [per_device(): summed, down_projected = lax.psum((partial_value, shrink_part), 'tensor')]
    slice x3 -> x0, local copies, waits for them, and re-layouts: 3.31 us -> none  [the longest x1 2.37 us: per_device(): down_send[offset]]
    sub x1 -> x0, other arithmetic: 2.61 us -> none  [per_device(): asked - 1]
  transfers between devices with their start and end apart: 10 -> 0, of which waited for: 4 -> 0; matrix products, arithmetic and copies ran while one was open for 13% -> 0% of each run, Pallas kernels for 0% -> 0%
where the time goes in v1:
time: 50.1 us; the launch traced here: 50 us
  Pallas kernels  47.7 us (95%)
  local copies, waits for them, and re-layouts  1.62 us (3%)
  between operations  0.66 us (1%)
    pallas_call x1, Pallas kernels, per_device(): pl.pallas_call(functools.partial(kernel, n_dp, n_tensor), name='adapted_p...  47.7 us
    unnamed x1, local copies, waits for them, and re-layouts  1.62 us

profile of v1, /device:TPU:1, one launch (start us, length us, event | category | flops | bytes accessed | tf_op | source)
XLA Modules:
  0.0 50.0 jit_solution(7478146977088319499)
XLA Ops:
  0.7 47.7 %adapted_projection.1 = bf16[768,128]{1,0:T(8,128)(2,1)} custom-call(bf16[6,128,1024]{2,1,0:T(8,128)(2,1)} %bitcast.1, bf16[1024,1024]{1,0:T(8,128)(2,1)} %w_hbm.1, bf16[4,64,1024]{2,1,0:T(8,128)(2,1)} %down_hbm.1, bf16[4,64,128]{2,1,0:T(8,128)(2,1)} %up_hbm.1, s32[256]{0:T(256)} %slot_hbm.1, s32[6]{0:T(128)} %ids_hbm.1, s32[1]{0:T(128)S(6)} %copy.9.live_hbm), custom_call_target="tpu_custom_call" | custom-call | flops 2000000000 | bytes 4500000 | tf_op jit(solution)/shard_map/adapted_projection/pallas_call | solution.py:349
  48.4 1.6 %copy.10 = bf16[768,128]{1,0:T(8,128)(2,1)} copy(bf16[768,128]{1,0:T(8,128)(2,1)} %adapted_projection.1) | data formatting | bytes 393216

commit v2 on v1

--- a/solution.py
+++ b/solution.py
@@ -14,9 +14,10 @@
 RING = 8
 SEG = 128
 RANK = 64
-DIRECT = 32
+DIRECT = 16
 PIECE = 16
 PIECES = (RANK - DIRECT) // PIECE
+STEP = 3
 ORDER = (2, 1, 3, 0)
 
 
@@ -61,11 +62,15 @@
     x_out,
     x_in,
     s_mine,
+    s_core,
     s_out,
     s_in,
+    s_all,
     t_mine,
+    t_core,
     t_out,
     t_in,
+    t_all,
     acc,
     load_sem,
     req_send,
@@ -91,6 +96,8 @@
     t = lax.axis_index("tensor")
     n_chip = n_tensor // 2
     segs = tok.shape[0]
+    half = segs // 2
+    core = lax.rem(t, 2)
     stored = down.shape[0]
 
     def dp_at(offset):
@@ -99,7 +106,7 @@
     def tensor_at(offset):
         return (me, lax.rem(t + offset, n_tensor))
 
-    other_core = (me, t + 1 - 2 * lax.rem(t, 2))
+    other_core = (me, t + 1 - 2 * core)
     row = me // RING * RING
     y = lax.rem(me, RING)
     relay_to = (row + lax.rem(y + 2, RING), t)
@@ -129,14 +136,14 @@
     tok_load = pltpu.make_async_copy(tokens_hbm, tok, load_sem.at[5])
     w_load = []
     for i, k in enumerate(ORDER):
-        for half in range(2):
+        for side in range(2):
             owner = lax.rem(t + 2 * k, n_tensor)
-            if half:
+            if side:
                 owner = owner + 1 - 2 * lax.rem(owner, 2)
             columns = pl.ds(pl.multiple_of(owner * 128, 128), 128)
             w_load.append(
                 pltpu.make_async_copy(
-                    w_hbm.at[:, columns], w.at[i, :, pl.ds(half * 128, 128)], load_sem.at[6 + 2 * i + half]
+                    w_hbm.at[:, columns], w.at[i, :, pl.ds(side * 128, 128)], load_sem.at[6 + 2 * i + side]
                 )
             )
     for copy in small:
@@ -175,24 +182,26 @@
     for copy in asks:
         copy.start()
 
-    core_copies = []
+    core_copies, x_copies, a_copies, relay_copies, pass_copies, b_copies = [], [], [], [], [], []
 
     def base_block(i):
         w_load[2 * i].wait()
         w_load[2 * i + 1].wait()
-
-        def rows(s, carry):
-            part = jnp.dot(tok[s], w[i], preferred_element_type=F32)
-            mine[i, s] = part[:, :128]
-            core_out[i, s] = part[:, 128:]
-            return carry
-
-        lax.fori_loop(0, segs, rows, 0)
+        for s in range(0, segs, STEP):
+            rows = tok[pl.ds(s, STEP)].reshape(STEP * SEG, tok.shape[2])
+            part = jnp.dot(rows, w[i], preferred_element_type=F32)
+            mine[i, pl.ds(s * SEG, STEP * SEG), :] = part[:, :128]
+            core_out[i, pl.ds(s * SEG, STEP * SEG), :] = part[:, 128:]
         copy = remote(core_out.at[i], core_in.at[i], core_send.at[i], core_recv.at[i], other_core)
         copy.start()
         core_copies.append(copy)
 
-    a_copies, relay_copies, b_copies = [], [], []
+    def base_send(i):
+        core_copies[i].wait_recv()
+        x_out[i] = (mine[i] + core_in[i]).astype(BF16)
+        copy = remote(x_out.at[i], x_in.at[i], x_send.at[i], x_recv.at[i], tensor_at(2 * ORDER[i]))
+        copy.start()
+        x_copies.append(copy)
 
     def serve(o):
         asks[o - 1].wait_recv()
@@ -201,11 +210,6 @@
         b_out[o - 1] = up[pick]
         dst = a_near.at[o] if o < 3 else a_far
         rows = RANK if o < 3 else DIRECT
-        copy = remote(
-            a_out.at[o - 1, pl.ds(0, rows)], dst.at[pl.ds(0, rows)], a_send.at[o - 1], a_recv.at[o - 1], dp_at(-o)
-        )
-        copy.start()
-        a_copies.append(copy)
         if o == 3:
             for j in range(PIECES):
                 copy = remote(
@@ -217,6 +221,11 @@
                 )
                 copy.start()
                 relay_copies.append(copy)
+        copy = remote(
+            a_out.at[o - 1, pl.ds(0, rows)], dst.at[pl.ds(0, rows)], a_send.at[o - 1], a_recv.at[o - 1], dp_at(-o)
+        )
+        copy.start()
+        a_copies.append(copy)
 
     tok_load.wait()
     base_block(0)
@@ -224,22 +233,16 @@
     up_load.wait()
     a_near[0] = down[wanted[0]]
     b_near[0] = twice(up[wanted[0]])
+    serve(1)
     base_block(1)
-    serve(1)
-    base_block(2)
     serve(2)
     serve(3)
+    base_send(0)
+    base_block(2)
+    base_send(1)
     base_block(3)
-
-    x_copies = []
-    for i in range(3):
-        core_copies[i].wait_recv()
-        x_out[i] = (mine[i] + core_in[i]).astype(BF16)
-        copy = remote(x_out.at[i], x_in.at[i], x_send.at[i], x_recv.at[i], tensor_at(2 * ORDER[i]))
-        copy.start()
-        x_copies.append(copy)
-
-    pass_copies = []
+    base_send(2)
+
     for j in range(PIECES):
         relay_copies[j].wait_recv()
         copy = remote(
@@ -254,8 +257,41 @@
         copy.start()
         b_copies.append(copy)
 
+    def rows_of(part, owner):
+        size = part.shape[0] // 2
+        return part.at[pl.ds(pl.multiple_of(owner * size, size), size)]
+
+    def core_phase(part, landing, sems):
+        copy = remote(rows_of(part, 1 - core), landing, sems[0].at[0], sems[1].at[0], other_core)
+        copy.start()
+        return [copy]
+
+    def chip_phase(part, landing, out, arrived, sems, copies):
+        copies[0].wait_recv()
+        landing[...] = rows_of(part, core)[...] + landing[...]
+        out[...] = landing[...].astype(BF16)
+        for k in range(1, n_chip):
+            copy = remote(out, arrived.at[k - 1], sems[0].at[k], sems[1].at[k], tensor_at(2 * k))
+            copy.start()
+            copies.append(copy)
+
+    def swap_phase(landing, arrived, total, sems, copies):
+        for k in range(1, n_chip):
+            copies[k].wait_recv()
+        rows = landing[...]
+        for k in range(1, n_chip):
+            rows = rows + arrived[k - 1].astype(F32)
+        rows_of(total, core)[...] = rows.astype(BF16)
+        copy = remote(
+            rows_of(total, core), rows_of(total, core), sems[0].at[n_chip], sems[1].at[n_chip], other_core
+        )
+        copy.start()
+        copies.append(copy)
+
     low_lanes = lax.broadcasted_iota(jnp.int32, (SEG, 128), 1) < RANK
-    half = segs // 2
+
+    def seg_rows(s):
+        return pl.ds(s * SEG, SEG)
 
     a_copies[0].wait_recv()
     a_copies[1].wait_recv()
@@ -264,14 +300,10 @@
         return nt_dot(tok[s], twice(a_near[jnp.minimum(offs[s], 2)]))
 
     for j in range(half):
-        packed = jnp.where(low_lanes, near_shrink(j), near_shrink(j + half))
-        s_mine[j] = packed
-        s_out[j] = packed.astype(BF16)
-    s_copies = []
-    for k in range(1, n_tensor):
-        copy = remote(s_out, s_in.at[k - 1], s_send.at[k - 1], s_recv.at[k - 1], tensor_at(k))
-        copy.start()
-        s_copies.append(copy)
+        s_mine[seg_rows(j), :] = jnp.where(low_lanes, near_shrink(j), near_shrink(j + half))
+    s_sems, t_sems = (s_send, s_recv), (t_send, t_recv)
+    s_copies = core_phase(s_mine, s_core, s_sems)
+    chip_phase(s_mine, s_core, s_out, s_in, s_sems, s_copies)
 
     a_copies[2].wait_recv()
     for copy in pass_copies:
@@ -281,51 +313,39 @@
     second = nt_dot(tok[segs - 2], far)
     third = nt_dot(tok[segs - 1], far)
     h = SEG // 2
-    packed = jnp.concatenate(
-        [jnp.where(low_lanes, first, second), jnp.where(low_lanes[:h], third[:h], third[h:])], axis=0
-    )
-    t_mine[...] = packed
-    t_out[...] = packed.astype(BF16)
-    t_copies = []
-    for k in range(1, n_tensor):
-        copy = remote(t_out, t_in.at[k - 1], t_send.at[k - 1], t_recv.at[k - 1], tensor_at(k))
-        copy.start()
-        t_copies.append(copy)
+    t_mine[pl.ds(0, SEG), :] = jnp.where(low_lanes, first, second)
+    t_mine[pl.ds(SEG, h), :] = jnp.where(low_lanes[:h], third[:h], third[h:])
+    t_copies = core_phase(t_mine, t_core, t_sems)
 
     core_copies[3].wait_recv()
     for copy in x_copies:
         copy.wait_recv()
-    acc[...] = (
-        mine[3] + core_in[3] + x_in[0].astype(F32) + x_in[1].astype(F32) + x_in[2].astype(F32)
-    )
+    acc[...] = mine[3] + core_in[3] + x_in[0].astype(F32) + x_in[1].astype(F32) + x_in[2].astype(F32)
+
+    chip_phase(t_mine, t_core, t_out, t_in, t_sems, t_copies)
+    swap_phase(s_core, s_in, s_all, s_sems, s_copies)
 
     b_copies[0].wait_recv()
     b_copies[1].wait_recv()
     for o in (1, 2):
         b_near[o, RANK:] = b_near[o, :RANK]
-    for copy in s_copies:
-        copy.wait_recv()
+    s_copies[-1].wait_recv()
     for j in range(half):
-        total = s_mine[j]
-        for k in range(n_tensor - 1):
-            total = total + s_in[k, j].astype(F32)
+        total = s_all[seg_rows(j), :]
         for s, keep in ((j, low_lanes), (j + half, ~low_lanes)):
-            x = jnp.where(keep, total, 0.0).astype(BF16)
+            x = jnp.where(keep, total, jnp.zeros_like(total))
             add = jnp.dot(x, b_near[jnp.minimum(offs[s], 2)], preferred_element_type=F32)
             used = (offs[s] < 3) & (s < live_count)
-            acc[s] += jnp.where(used, add, 0.0)
+            acc[seg_rows(s), :] += jnp.where(used, add, 0.0)
 
     b_copies[2].wait_recv()
     bf = twice(b_far[...])
-    for copy in t_copies:
-        copy.wait_recv()
-    total = t_mine[...]
-    for k in range(n_tensor - 1):
-        total = total + t_in[k].astype(F32)
-    top, low = total[:SEG], total[SEG:]
+    swap_phase(t_core, t_in, t_all, t_sems, t_copies)
+    t_copies[-1].wait_recv()
+    top, low = t_all[pl.ds(0, SEG), :], t_all[pl.ds(SEG, h), :]
 
     def far_delta(x, keep):
-        return jnp.dot(jnp.where(keep, x, 0.0).astype(BF16), bf, preferred_element_type=F32)
+        return jnp.dot(jnp.where(keep, x, jnp.zeros_like(x)), bf, preferred_element_type=F32)
 
     first = far_delta(top, low_lanes)
     second = far_delta(top, ~low_lanes)
@@ -333,7 +353,7 @@
     for s in range(segs):
         add = first if s < 4 else second if s == segs - 2 else third
         used = (offs[s] == 3) & (s < live_count)
-        out_ref[pl.ds(s * SEG, SEG), :] = (acc[s] + jnp.where(used, add, 0.0)).astype(out_ref.dtype)
+        out_ref[seg_rows(s), :] = (acc[seg_rows(s), :] + jnp.where(used, add, 0.0)).astype(out_ref.dtype)
 
     for copy in asks + a_copies + relay_copies + pass_copies + b_copies + core_copies + x_copies + s_copies + t_copies:
         copy.wait_send()
@@ -343,13 +363,14 @@
     rows, width = tokens.shape
     segs = ids.shape[0]
     stored, rank, columns = up.shape
-    peers = n_tensor - 1
+    chips = n_tensor // 2
+    near, far = rows // 2, SEG + SEG // 2
     dma = pltpu.SemaphoreType.DMA
     vmem, smem = pltpu.VMEM, pltpu.SMEM
     return pl.pallas_call(
         functools.partial(kernel, n_dp, n_tensor),
         name="adapted_projection",
-        out_shape=jax.ShapeDtypeStruct((rows, columns), BF16),
+        out_shape=pltpu.VMEM((rows, columns), BF16),
         in_specs=[pl.BlockSpec(memory_space=pl.ANY)] * 7,
         out_specs=pl.BlockSpec(memory_space=pltpu.VMEM),
         scratch_shapes=[
@@ -369,18 +390,22 @@
             vmem((3, rank, columns), BF16),
             vmem((3, 2 * rank, columns), BF16),
             vmem((rank, columns), BF16),
-            vmem((4, segs, SEG, columns), F32),
-            vmem((4, segs, SEG, columns), F32),
-            vmem((4, segs, SEG, columns), F32),
-            vmem((3, segs, SEG, columns), BF16),
-            vmem((3, segs, SEG, columns), BF16),
-            vmem((segs // 2, SEG, 128), F32),
-            vmem((segs // 2, SEG, 128), BF16),
-            vmem((peers, segs // 2, SEG, 128), BF16),
-            vmem((SEG + SEG // 2, 128), F32),
-            vmem((SEG + SEG // 2, 128), BF16),
-            vmem((peers, SEG + SEG // 2, 128), BF16),
-            vmem((segs, SEG, columns), F32),
+            vmem((4, rows, columns), F32),
+            vmem((4, rows, columns), F32),
+            vmem((4, rows, columns), F32),
+            vmem((3, rows, columns), BF16),
+            vmem((3, rows, columns), BF16),
+            vmem((near, 128), F32),
+            vmem((near // 2, 128), F32),
+            vmem((near // 2, 128), BF16),
+            vmem((chips - 1, near // 2, 128), BF16),
+            vmem((near, 128), BF16),
+            vmem((far, 128), F32),
+            vmem((far // 2, 128), F32),
+            vmem((far // 2, 128), BF16),
+            vmem((chips - 1, far // 2, 128), BF16),
+            vmem((far, 128), BF16),
+            vmem((rows, columns), F32),
             dma((14,)),
             dma((3,)),
             dma((3,)),
@@ -396,10 +421,10 @@
             dma((4,)),
             dma((3,)),
             dma((3,)),
-            dma((peers,)),
-            dma((peers,)),
-            dma((peers,)),
-            dma((peers,)),
+            dma((chips + 1,)),
+            dma((chips + 1,)),
+            dma((chips + 1,)),
+            dma((chips + 1,)),
         ],
         compiler_params=pltpu.CompilerParams(
             collective_id=0, has_side_effects=True, vmem_limit_bytes=63 * 1024 * 1024

time: 50.1 us -> 41.7 us (0.83)
  Pallas kernels: 47.7 us -> 40.1 us
  local copies, waits for them, and re-layouts: 1.62 us -> 0.68 us
    pallas_call x1, Pallas kernels: 47.7 us -> 40.1 us  [per_device(): pl.pallas_call(functools.partial(kernel, n_dp, n_tensor), name='adapted_p...]
    unnamed x1, local copies, waits for them, and re-layouts: 1.62 us -> 0.68 us
where the time goes in v2:
time: 41.7 us; the launch traced here: 41.5 us
  Pallas kernels  40.1 us (96%)
  local copies, waits for them, and re-layouts  0.68 us (2%)
  between operations  0.66 us (2%)
    pallas_call x1, Pallas kernels, per_device(): pl.pallas_call(functools.partial(kernel, n_dp, n_tensor), name='adapted_p...  40.1 us

profile of v2, /device:TPU:1, one launch (start us, length us, event | category | flops | bytes accessed | tf_op | source)
XLA Modules:
  0.0 41.5 jit_solution(7779421767474517464)
XLA Ops:
  0.7 40.1 %adapted_projection.1 = bf16[768,128]{1,0:T(8,128)(2,1)S(1)} custom-call(bf16[6,128,1024]{2,1,0:T(8,128)(2,1)} %bitcast.1, bf16[1024,1024]{1,0:T(8,128)(2,1)} %w_hbm.1, bf16[4,64,1024]{2,1,0:T(8,128)(2,1)} %down_hbm.1, bf16[4,64,128]{2,1,0:T(8,128)(2,1)} %up_hbm.1, s32[256]{0:T(256)} %slot_hbm.1, s32[6]{0:T(128)} %ids_hbm.1, s32[1]{0:T(128)S(6)} %copy.10.live_hbm), custom_call_target="tpu_custom_call" | custom-call | flops 2000000000 | bytes 4500000 | tf_op jit(solution)/shard_map/adapted_projection/pallas_call | solution.py:370
  40.8 0.7 %copy.9 = bf16[768,128]{1,0:T(8,128)(2,1)} copy(bf16[768,128]{1,0:T(8,128)(2,1)S(1)} %adapted_projection.1) | data formatting | bytes 393216

commit v3 on v2

v3 whole, which is shorter than its diff:
```python
import functools

import jax
import jax.numpy as jnp
from jax import lax
from jax.experimental import pallas as pl
from jax.experimental.pallas import tpu as pltpu
from jax.sharding import PartitionSpec as P

MESH = pl.DeviceIdType.MESH
F32 = jnp.float32
BF16 = jnp.bfloat16

RING = 8
SEG = 128
RANK = 64
HALF = RANK // 2
SHORT = 384
PIECES = ((384, 256), (640, 384))
GROUPS = 128 // HALF
STEP = 3
ORDER = (2, 1, 3, 0)


def nt_dot(a, b):
    return lax.dot_general(a, b, (((1,), (1,)), ((), ())), preferred_element_type=F32)


def kernel(
    n_dp,
    n_tensor,
    tokens_hbm,
    w_hbm,
    down_hbm,
    up_hbm,
    slot_hbm,
    ids_hbm,
    live_hbm,
    out_ref,
    tok,
    tok_other,
    w,
    down,
    up,
    slot,
    ids,
    live,
    req_out,
    req_in,
    a_out,
    a_in,
    relay,
    b_out,
    b_in,
    b_relay,
    mine,
    core_out,
    core_in,
    x_out,
    x_in,
    s_mine,
    s_out,
    s_in,
    s_all,
    acc,
    load_sem,
    req_send,
    req_recv,
    a_send,
    a_recv,
    swap_send,
    swap_recv,
    relay_send,
    relay_recv,
    pass_send,
    pass_recv,
    b_send,
    b_recv,
    core_send,
    core_recv,
    x_send,
    x_recv,
    s_send,
    s_recv,
):
    me = lax.axis_index("dp")
    t = lax.axis_index("tensor")
    n_chip = n_tensor // 2
    segs = tok.shape[0]
    stored = down.shape[0]

    core = lax.rem(t, 2)
    sides = (t, t + 1 - 2 * core)

    def dp_at(offset, cross=0):
        return (lax.rem(me + offset + n_dp, n_dp), sides[cross])

    def tensor_at(offset):
        return (me, lax.rem(t + offset, n_tensor))

    other_core = (me, sides[1])
    row = me // RING * RING
    y = lax.rem(me, RING)
    relay_to = (row + lax.rem(y + 2, RING), t)
    relay_from = (row + lax.rem(y + RING - 2, RING), t)
    pass_index = lax.rem(row + lax.rem(y + RING - 2, RING) - 3 + n_dp, n_dp)
    pass_to = [(pass_index, side) for side in sides]
    far_owner = lax.rem(me + 3, n_dp)
    from_index = far_owner // RING * RING + lax.rem(lax.rem(far_owner, RING) + 2, RING)
    pass_from = [(from_index, side) for side in sides]

    def remote(src, dst, send, recv, device):
        return pltpu.make_async_remote_copy(
            src_ref=src, dst_ref=dst, send_sem=send, recv_sem=recv, device_id=device, device_id_type=MESH
        )

    barrier = pltpu.get_barrier_semaphore()
    peers = [dp_at(o, cross) for o in (1, 2, 3, -1, -2, -3) for cross in range(2)]
    peers += [relay_to, relay_from, *pass_to, *pass_from]
    peers += [tensor_at(k) for k in range(1, n_tensor)]
    for peer in peers:
        pl.semaphore_signal(barrier, inc=1, device_id=peer, device_id_type=MESH)

    small = [
        pltpu.make_async_copy(src, dst, load_sem.at[i])
        for i, (src, dst) in enumerate(((slot_hbm, slot), (ids_hbm, ids), (live_hbm, live)))
    ]
    down_load = pltpu.make_async_copy(down_hbm, down, load_sem.at[3])
    up_load = pltpu.make_async_copy(up_hbm, up, load_sem.at[4])
    tok_load = pltpu.make_async_copy(tokens_hbm, tok, load_sem.at[5])
    w_load = []
    for i, k in enumerate(ORDER):
        for side in range(2):
            owner = lax.rem(t + 2 * k, n_tensor)
            if side:
                owner = owner + 1 - 2 * lax.rem(owner, 2)
            columns = pl.ds(pl.multiple_of(owner * 128, 128), 128)
            w_load.append(
                pltpu.make_async_copy(
                    w_hbm.at[:, columns], w.at[i, :, pl.ds(side * 128, 128)], load_sem.at[6 + 2 * i + side]
                )
            )
    for copy in small:
        copy.start()
    down_load.start()
    tok_load.start()
    for copy in w_load:
        copy.start()
    up_load.start()

    for copy in small:
        copy.wait()
    offs, locs = [], []
    for s in range(segs):
        place = slot[ids[s]]
        offs.append(lax.rem(place // stored - me + n_dp, n_dp))
        locs.append(lax.rem(place, stored))
    wanted = []
    for o in range(4):
        found = jnp.int32(0)
        for s in range(4):
            found = jnp.where(offs[s] == o, locs[s], found)
        wanted.append(found)
    far_seg = jnp.int32(0)
    for s in range(4):
        far_seg = jnp.where(offs[s] == 3, s, far_seg)
    live_count = live[0]
    for o in range(1, 4):
        req_out[o - 1] = jnp.full(req_out.shape[1:], wanted[o], jnp.int32)

    pl.semaphore_wait(barrier, len(peers))
    asks = [
        remote(req_out.at[o - 1], req_in.at[o - 1], req_send.at[o - 1], req_recv.at[o - 1], dp_at(o))
        for o in range(1, 4)
    ]
    for copy in asks:
        copy.start()

    core_copies, x_copies, a_copies, swap_copies, relay_copies, pass_copies, b_copies = [], [], [], [], [], [], []

    def base_block(i):
        w_load[2 * i].wait()
        w_load[2 * i + 1].wait()
        for s in range(0, segs, STEP):
            rows = tok[pl.ds(s, STEP)].reshape(STEP * SEG, tok.shape[2])
            part = jnp.dot(rows, w[i], preferred_element_type=F32)
            mine[i, pl.ds(s * SEG, STEP * SEG), :] = part[:, :128]
            core_out[i, pl.ds(s * SEG, STEP * SEG), :] = part[:, 128:]
        copy = remote(core_out.at[i], core_in.at[i], core_send.at[i], core_recv.at[i], other_core)
        copy.start()
        core_copies.append(copy)

    def base_send(i):
        core_copies[i].wait_recv()
        x_out[i] = (mine[i] + core_in[i]).astype(BF16)
        copy = remote(x_out.at[i], x_in.at[i], x_send.at[i], x_recv.at[i], tensor_at(2 * ORDER[i]))
        copy.start()
        x_copies.append(copy)

    def start(copies, *what):
        copy = remote(*what)
        copy.start()
        copies.append(copy)

    def rank_half(cross):
        start_row = (1 - core) * HALF if cross else core * HALF
        return pl.ds(pl.multiple_of(start_row, HALF), HALF)

    def serve(o, crosses=(0, 1), again=False):
        if not again:
            asks[o - 1].wait_recv()
            pick = jnp.max(req_in[o - 1])
            a_out[o] = down[pick]
            b_out[o - 1] = up[pick]
        if o == 3:
            for p, (first, size) in enumerate(PIECES):
                for cross in range(2):
                    n = 2 * p + cross
                    src = a_out.at[o, rank_half(cross), pl.ds(first, size)]
                    start(relay_copies, src, relay.at[cross, :, pl.ds(first - SHORT, size)], relay_send.at[n], relay_recv.at[n], relay_to)
        for cross in crosses:
            lanes = pl.ds(0, a_out.shape[2] if o < 3 else SHORT)
            src = a_out.at[o, rank_half(cross), lanes]
            n = 2 * (o - 1) + cross
            start(a_copies, src, a_in.at[o, cross, :, lanes], a_send.at[n], a_recv.at[n], dp_at(-o, cross))

    def pass_on(p, cross):
        n = 2 * p + cross
        relay_copies[n].wait_recv()
        first, size = PIECES[p]
        src = relay.at[cross, :, pl.ds(first - SHORT, size)]
        dst = a_in.at[3, cross, :, pl.ds(first, size)]
        start(pass_copies, src, dst, pass_send.at[n], pass_recv.at[n], pass_to[cross])

    tok_load.wait()
    base_block(0)
    down_load.wait()
    up_load.wait()
    a_out[0] = down[wanted[0]]
    a_in[0, 0] = a_out[0, rank_half(0)]
    b_in[0] = up[wanted[0]]
    serve(1, (0,))
    base_block(1)
    serve(2, (0,))
    serve(3)
    serve(2, (1,), True)
    serve(1, (1,), True)
    base_send(0)
    base_block(2)
    base_send(1)
    base_block(3)
    base_send(2)
    start(swap_copies, tok, tok_other, swap_send.at[0], swap_recv.at[0], other_core)
    start(swap_copies, a_out.at[0, rank_half(1)], a_in.at[0, 1], swap_send.at[1], swap_recv.at[1], other_core)
    for p in range(len(PIECES)):
        for cross in range(2):
            pass_on(p, cross)
    n = 2 * len(PIECES)
    start(relay_copies, b_out.at[2], b_relay, relay_send.at[n], relay_recv.at[n], relay_to)

    lane_group = lax.broadcasted_iota(jnp.int32, (SEG, 128), 1) // HALF
    row_group = lax.broadcasted_iota(jnp.int32, (SEG, 128), 0) // HALF
    own_group = lane_group == row_group

    def spread(a):
        return jnp.concatenate([a] * GROUPS, axis=0)

    for copy in swap_copies + a_copies + pass_copies:
        copy.wait_recv()
    for s in range(segs):
        o = jnp.minimum(offs[s], 3)
        part = nt_dot(tok[s], spread(a_in[o, 0])) + nt_dot(tok_other[s], spread(a_in[o, 1]))
        kept = jnp.where(own_group, part, 0.0)
        packed = kept[:HALF]
        for g in range(1, GROUPS):
            packed = packed + kept[g * HALF : (g + 1) * HALF]
        s_mine[s] = packed
        s_out[s] = packed.astype(BF16)
    s_copies = []
    for k in range(1, n_chip):
        start(s_copies, s_out, s_in.at[k - 1], s_send.at[k - 1], s_recv.at[k - 1], tensor_at(2 * k))

    for o in (1, 2):
        start(b_copies, b_out.at[o - 1], b_in.at[o], b_send.at[o - 1], b_recv.at[o - 1], dp_at(-o))
    relay_copies[n].wait_recv()
    start(b_copies, b_relay, b_in.at[3], b_send.at[2], b_recv.at[2], pass_to[0])

    core_copies[3].wait_recv()
    for copy in x_copies:
        copy.wait_recv()
    acc[...] = mine[3] + core_in[3] + x_in[0].astype(F32) + x_in[1].astype(F32) + x_in[2].astype(F32)

    for copy in s_copies:
        copy.wait_recv()
    total = s_mine[...]
    for k in range(n_chip - 1):
        total = total + s_in[k].astype(F32)
    s_all[core] = total.astype(BF16)
    start(s_copies, s_all.at[core], s_all.at[core], s_send.at[n_chip - 1], s_recv.at[n_chip - 1], other_core)

    for copy in b_copies:
        copy.wait_recv()
    s_copies[-1].wait_recv()
    for s in range(segs):
        factor = b_in[jnp.minimum(offs[s], 3)]
        add = None
        for h in range(2):
            x = jnp.where(own_group, spread(s_all[h, s].astype(F32)), 0.0).astype(BF16)
            term = jnp.dot(x, spread(factor[h * HALF : (h + 1) * HALF]), preferred_element_type=F32)
            add = term if add is None else add + term
        add = jnp.where(s < live_count, add, 0.0)
        rows = pl.ds(s * SEG, SEG)
        out_ref[rows, :] = (acc[rows, :] + add).astype(out_ref.dtype)

    for copy in asks + a_copies + swap_copies + relay_copies + pass_copies + b_copies + core_copies + x_copies + s_copies:
        copy.wait_send()


def per_device(n_dp, n_tensor, tokens, w, down, up, slot, ids, live):
    rows, width = tokens.shape
    segs = ids.shape[0]
    stored, rank, columns = up.shape
    chips = n_tensor // 2
    dma = pltpu.SemaphoreType.DMA
    vmem, smem = pltpu.VMEM, pltpu.SMEM
    return pl.pallas_call(
        functools.partial(kernel, n_dp, n_tensor),
        name="adapted_projection",
        out_shape=pltpu.VMEM((rows, columns), BF16),
        in_specs=[pl.BlockSpec(memory_space=pl.ANY)] * 7,
        out_specs=pl.BlockSpec(memory_space=pltpu.VMEM),
        scratch_shapes=[
            vmem((segs, SEG, width), BF16),
            vmem((segs, SEG, width), BF16),
            vmem((4, width, 2 * columns), BF16),
            vmem((stored, rank, width), BF16),
            vmem((stored, rank, columns), BF16),
            smem(slot.shape, jnp.int32),
            smem(ids.shape, jnp.int32),
            smem(live.shape, jnp.int32),
            vmem((3, 8, 128), jnp.int32),
            vmem((3, 8, 128), jnp.int32),
            vmem((4, rank, width), BF16),
            vmem((4, 2, HALF, width), BF16),
            vmem((2, HALF, width - SHORT), BF16),
            vmem((3, rank, columns), BF16),
            vmem((4, rank, columns), BF16),
            vmem((rank, columns), BF16),
            vmem((4, rows, columns), F32),
            vmem((4, rows, columns), F32),
            vmem((4, rows, columns), F32),
            vmem((3, rows, columns), BF16),
            vmem((3, rows, columns), BF16),
            vmem((segs, HALF, 128), F32),
            vmem((segs, HALF, 128), BF16),
            vmem((chips - 1, segs, HALF, 128), BF16),
            vmem((2, segs, HALF, 128), BF16),
            vmem((rows, columns), F32),
            dma((14,)),
            dma((3,)),
            dma((3,)),
            dma((6,)),
            dma((6,)),
            dma((2,)),
            dma((2,)),
            dma((2 * len(PIECES) + 1,)),
            dma((2 * len(PIECES) + 1,)),
            dma((2 * len(PIECES),)),
            dma((2 * len(PIECES),)),
            dma((3,)),
            dma((3,)),
            dma((4,)),
            dma((4,)),
            dma((3,)),
            dma((3,)),
            dma((chips,)),
            dma((chips,)),
        ],
        compiler_params=pltpu.CompilerParams(
            collective_id=0, has_side_effects=True, vmem_limit_bytes=63 * 1024 * 1024
        ),
        cost_estimate=pl.CostEstimate(flops=2_000_000_000, bytes_accessed=4_500_000, transcendentals=0),
    )(tokens.reshape(segs, SEG, width), w, down, up, slot, ids, live)


def solution(mesh):
    placed = (
        P("dp", "tensor"),
        P("tensor", None),
        P("dp", None, "tensor"),
        P("dp", None, "tensor"),
        P(),
        P("dp"),
        P("dp"),
    )
    return jax.shard_map(
        functools.partial(per_device, mesh.shape["dp"], mesh.shape["tensor"]),
        mesh=mesh,
        in_specs=placed,
        out_specs=P("dp", "tensor"),
        check_vma=False,
    )
```

time: 41.7 us -> 41.4 us (level)
  no operation moved by 1% of the time
where the time goes in v3:
time: 41.4 us; the launch traced here: 41.3 us
  Pallas kernels  40 us (97%)
  local copies, waits for them, and re-layouts  0.68 us (2%)
  between operations  0.66 us (2%)
    pallas_call x1, Pallas kernels, per_device(): pl.pallas_call(functools.partial(kernel, n_dp, n_tensor), name='adapted_p...  40 us

profile of v3, /device:TPU:1, one launch (start us, length us, event | category | flops | bytes accessed | tf_op | source)
XLA Modules:
  0.0 41.3 jit_solution(10728488275550560736)
XLA Ops:
  0.7 40.0 %adapted_projection.1 = bf16[768,128]{1,0:T(8,128)(2,1)S(1)} custom-call(bf16[6,128,1024]{2,1,0:T(8,128)(2,1)} %bitcast.1, bf16[1024,1024]{1,0:T(8,128)(2,1)} %w_hbm.1, bf16[4,64,1024]{2,1,0:T(8,128)(2,1)} %down_hbm.1, bf16[4,64,128]{2,1,0:T(8,128)(2,1)} %up_hbm.1, s32[256]{0:T(256)} %slot_hbm.1, s32[6]{0:T(128)} %ids_hbm.1, s32[1]{0:T(128)S(6)} %copy.10.live_hbm), custom_call_target="tpu_custom_call" | custom-call | flops 2000000000 | bytes 4500000 | tf_op jit(solution)/shard_map/adapted_projection/pallas_call | solution.py:326
  40.6 0.7 %copy.9 = bf16[768,128]{1,0:T(8,128)(2,1)} copy(bf16[768,128]{1,0:T(8,128)(2,1)S(1)} %adapted_projection.1) | data formatting | bytes 393216

commit v4 on v3

--- a/solution.py
+++ b/solution.py
@@ -105,9 +105,6 @@
     relay_from = (row + lax.rem(y + RING - 2, RING), t)
     pass_index = lax.rem(row + lax.rem(y + RING - 2, RING) - 3 + n_dp, n_dp)
     pass_to = [(pass_index, side) for side in sides]
-    far_owner = lax.rem(me + 3, n_dp)
-    from_index = far_owner // RING * RING + lax.rem(lax.rem(far_owner, RING) + 2, RING)
-    pass_from = [(from_index, side) for side in sides]
 
     def remote(src, dst, send, recv, device):
         return pltpu.make_async_remote_copy(
@@ -115,8 +112,7 @@
         )
 
     barrier = pltpu.get_barrier_semaphore()
-    peers = [dp_at(o, cross) for o in (1, 2, 3, -1, -2, -3) for cross in range(2)]
-    peers += [relay_to, relay_from, *pass_to, *pass_from]
+    peers = [dp_at(o) for o in (-1, -2, -3)] + [relay_from]
     peers += [tensor_at(k) for k in range(1, n_tensor)]
     for peer in peers:
         pl.semaphore_signal(barrier, inc=1, device_id=peer, device_id_type=MESH)
@@ -234,21 +230,21 @@
 
     tok_load.wait()
     base_block(0)
+    base_block(1)
     down_load.wait()
     up_load.wait()
     a_out[0] = down[wanted[0]]
     a_in[0, 0] = a_out[0, rank_half(0)]
     b_in[0] = up[wanted[0]]
+    base_block(2)
+    base_block(3)
+    base_send(0)
     serve(1, (0,))
-    base_block(1)
     serve(2, (0,))
     serve(3)
     serve(2, (1,), True)
     serve(1, (1,), True)
-    base_send(0)
-    base_block(2)
     base_send(1)
-    base_block(3)
     base_send(2)
     start(swap_copies, tok, tok_other, swap_send.at[0], swap_recv.at[0], other_core)
     start(swap_copies, a_out.at[0, rank_half(1)], a_in.at[0, 1], swap_send.at[1], swap_recv.at[1], other_core)

time: 41.4 us -> 39.3 us (0.949)
  the two profiles are of different devices: /device:TPU:1 before, /device:TPU:2 now
where the time goes in v4:
time: 39.3 us; the launch traced here: 39.2 us
  Pallas kernels  37.9 us (96%)
  local copies, waits for them, and re-layouts  0.68 us (2%)
  between operations  0.66 us (2%)
    pallas_call x1, Pallas kernels, per_device(): pl.pallas_call(functools.partial(kernel, n_dp, n_tensor), name='adapted_p...  37.9 us

profile of v4, /device:TPU:2, one launch (start us, length us, event | category | flops | bytes accessed | tf_op | source)
XLA Modules:
  0.0 39.2 jit_solution(9742101496007514066)
XLA Ops:
  0.7 37.9 %adapted_projection.1 = bf16[768,128]{1,0:T(8,128)(2,1)S(1)} custom-call(bf16[6,128,1024]{2,1,0:T(8,128)(2,1)} %bitcast.1, bf16[1024,1024]{1,0:T(8,128)(2,1)} %w_hbm.1, bf16[4,64,1024]{2,1,0:T(8,128)(2,1)} %down_hbm.1, bf16[4,64,128]{2,1,0:T(8,128)(2,1)} %up_hbm.1, s32[256]{0:T(256)} %slot_hbm.1, s32[6]{0:T(128)} %ids_hbm.1, s32[1]{0:T(128)S(6)} %copy.10.live_hbm), custom_call_target="tpu_custom_call" | custom-call | flops 2000000000 | bytes 4500000 | tf_op jit(solution)/shard_map/adapted_projection/pallas_call | solution.py:322
  38.5 0.7 %copy.9 = bf16[768,128]{1,0:T(8,128)(2,1)} copy(bf16[768,128]{1,0:T(8,128)(2,1)S(1)} %adapted_projection.1) | data formatting | bytes 393216

commit v5 on v4

--- a/solution.py
+++ b/solution.py
@@ -52,7 +52,6 @@
     relay,
     b_out,
     b_in,
-    b_relay,
     mine,
     core_out,
     core_in,
@@ -99,11 +98,12 @@
         return (me, lax.rem(t + offset, n_tensor))
 
     other_core = (me, sides[1])
-    row = me // RING * RING
-    y = lax.rem(me, RING)
-    relay_to = (row + lax.rem(y + 2, RING), t)
-    relay_from = (row + lax.rem(y + RING - 2, RING), t)
-    pass_index = lax.rem(row + lax.rem(y + RING - 2, RING) - 3 + n_dp, n_dp)
+
+    def far_relay(asker):
+        return asker // RING * RING + lax.rem(lax.rem(asker, RING) + 5, RING)
+
+    relay_to = (far_relay(lax.rem(me + n_dp - 3, n_dp)), t)
+    pass_index = me // RING * RING + lax.rem(lax.rem(me, RING) + RING - 5, RING)
     pass_to = [(pass_index, side) for side in sides]
 
     def remote(src, dst, send, recv, device):
@@ -112,7 +112,7 @@
         )
 
     barrier = pltpu.get_barrier_semaphore()
-    peers = [dp_at(o) for o in (-1, -2, -3)] + [relay_from]
+    peers = [dp_at(o) for o in (-1, -2, -3)] + [pass_to[0]]
     peers += [tensor_at(k) for k in range(1, n_tensor)]
     for peer in peers:
         pl.semaphore_signal(barrier, inc=1, device_id=peer, device_id_type=MESH)
@@ -172,7 +172,31 @@
     for copy in asks:
         copy.start()
 
-    core_copies, x_copies, a_copies, swap_copies, relay_copies, pass_copies, b_copies = [], [], [], [], [], [], []
+    core_copies, swap_copies, s_copies = [], [], []
+
+    def rank_half(cross):
+        start_row = (1 - core) * HALF if cross else core * HALF
+        return pl.ds(pl.multiple_of(start_row, HALF), HALF)
+
+    x_copies = [
+        remote(x_out.at[i], x_in.at[i], x_send.at[i], x_recv.at[i], tensor_at(2 * ORDER[i])) for i in range(3)
+    ]
+    a_copies, b_copies, relay_copies, pass_copies = [], [], [], []
+    for o in range(1, 4):
+        for cross in range(2):
+            lanes = pl.ds(0, a_out.shape[2] if o < 3 else SHORT)
+            n = 2 * (o - 1) + cross
+            src = a_out.at[o, rank_half(cross), lanes]
+            a_copies.append(remote(src, a_in.at[o, cross, :, lanes], a_send.at[n], a_recv.at[n], dp_at(-o, cross)))
+        b_copies.append(remote(b_out.at[o - 1], b_in.at[o], b_send.at[o - 1], b_recv.at[o - 1], dp_at(-o)))
+    for p, (first, size) in enumerate(PIECES):
+        for cross in range(2):
+            n = 2 * p + cross
+            src = a_out.at[3, rank_half(cross), pl.ds(first, size)]
+            here = relay.at[cross, :, pl.ds(first - SHORT, size)]
+            dst = a_in.at[3, cross, :, pl.ds(first, size)]
+            relay_copies.append(remote(src, here, relay_send.at[n], relay_recv.at[n], relay_to))
+            pass_copies.append(remote(here, dst, pass_send.at[n], pass_recv.at[n], pass_to[cross]))
 
     def base_block(i):
         w_load[2 * i].wait()
@@ -189,44 +213,62 @@
     def base_send(i):
         core_copies[i].wait_recv()
         x_out[i] = (mine[i] + core_in[i]).astype(BF16)
-        copy = remote(x_out.at[i], x_in.at[i], x_send.at[i], x_recv.at[i], tensor_at(2 * ORDER[i]))
-        copy.start()
-        x_copies.append(copy)
-
-    def start(copies, *what):
-        copy = remote(*what)
-        copy.start()
-        copies.append(copy)
-
-    def rank_half(cross):
-        start_row = (1 - core) * HALF if cross else core * HALF
-        return pl.ds(pl.multiple_of(start_row, HALF), HALF)
-
-    def serve(o, crosses=(0, 1), again=False):
-        if not again:
-            asks[o - 1].wait_recv()
-            pick = jnp.max(req_in[o - 1])
-            a_out[o] = down[pick]
-            b_out[o - 1] = up[pick]
+        x_copies[i].start()
+
+    def pick(o):
+        asks[o - 1].wait_recv()
+        asked = jnp.max(req_in[o - 1])
+        a_out[o] = down[asked]
+        b_out[o - 1] = up[asked]
+
+    def give(o, *crosses):
+        for cross in crosses:
+            a_copies[2 * (o - 1) + cross].start()
+
+    def serve(o):
+        pick(o)
         if o == 3:
-            for p, (first, size) in enumerate(PIECES):
-                for cross in range(2):
-                    n = 2 * p + cross
-                    src = a_out.at[o, rank_half(cross), pl.ds(first, size)]
-                    start(relay_copies, src, relay.at[cross, :, pl.ds(first - SHORT, size)], relay_send.at[n], relay_recv.at[n], relay_to)
-        for cross in crosses:
-            lanes = pl.ds(0, a_out.shape[2] if o < 3 else SHORT)
-            src = a_out.at[o, rank_half(cross), lanes]
-            n = 2 * (o - 1) + cross
-            start(a_copies, src, a_in.at[o, cross, :, lanes], a_send.at[n], a_recv.at[n], dp_at(-o, cross))
-
-    def pass_on(p, cross):
-        n = 2 * p + cross
-        relay_copies[n].wait_recv()
-        first, size = PIECES[p]
-        src = relay.at[cross, :, pl.ds(first - SHORT, size)]
-        dst = a_in.at[3, cross, :, pl.ds(first, size)]
-        start(pass_copies, src, dst, pass_send.at[n], pass_recv.at[n], pass_to[cross])
+            for copy in relay_copies:
+                copy.start()
+        give(o, 0, 1)
+        b_copies[o - 1].start()
+
+    def pass_on():
+        for there, onward in zip(relay_copies, pass_copies):
+            there.wait_recv()
+            onward.start()
+
+    def serve_all():
+        pick(1)
+        give(1, 0)
+        pick(2)
+        give(2, 0)
+        pick(3)
+        for copy in relay_copies:
+            copy.start()
+        give(3, 0, 1)
+        give(2, 1)
+        give(1, 1)
+        for copy in b_copies:
+            copy.start()
+        base_send(1)
+        base_send(2)
+        swap()
+        pass_on()
+
+    def serve_within(near):
+        for o in range(1, 1 + near):
+            serve(o)
+        base_send(1)
+        base_send(2)
+        swap()
+        pass_on()
+        for o in range(1 + near, 4):
+            serve(o)
+
+    def swap():
+        for copy in swap_copies:
+            copy.start()
 
     tok_load.wait()
     base_block(0)
@@ -239,20 +281,18 @@
     base_block(2)
     base_block(3)
     base_send(0)
-    serve(1, (0,))
-    serve(2, (0,))
-    serve(3)
-    serve(2, (1,), True)
-    serve(1, (1,), True)
-    base_send(1)
-    base_send(2)
-    start(swap_copies, tok, tok_other, swap_send.at[0], swap_recv.at[0], other_core)
-    start(swap_copies, a_out.at[0, rank_half(1)], a_in.at[0, 1], swap_send.at[1], swap_recv.at[1], other_core)
-    for p in range(len(PIECES)):
-        for cross in range(2):
-            pass_on(p, cross)
-    n = 2 * len(PIECES)
-    start(relay_copies, b_out.at[2], b_relay, relay_send.at[n], relay_recv.at[n], relay_to)
+    swap_copies.append(remote(tok, tok_other, swap_send.at[0], swap_recv.at[0], other_core))
+    swap_copies.append(remote(a_out.at[0, rank_half(1)], a_in.at[0, 1], swap_send.at[1], swap_recv.at[1], other_core))
+
+    @pl.when(me > 2)
+    def _():
+        serve_all()
+
+    for near in range(3):
+
+        @pl.when(me == near)
+        def _():
+            serve_within(near)
 
     lane_group = lax.broadcasted_iota(jnp.int32, (SEG, 128), 1) // HALF
     row_group = lax.broadcasted_iota(jnp.int32, (SEG, 128), 0) // HALF
@@ -272,14 +312,11 @@
             packed = packed + kept[g * HALF : (g + 1) * HALF]
         s_mine[s] = packed
         s_out[s] = packed.astype(BF16)
-    s_copies = []
     for k in range(1, n_chip):
-        start(s_copies, s_out, s_in.at[k - 1], s_send.at[k - 1], s_recv.at[k - 1], tensor_at(2 * k))
-
-    for o in (1, 2):
-        start(b_copies, b_out.at[o - 1], b_in.at[o], b_send.at[o - 1], b_recv.at[o - 1], dp_at(-o))
-    relay_copies[n].wait_recv()
-    start(b_copies, b_relay, b_in.at[3], b_send.at[2], b_recv.at[2], pass_to[0])
+        copy = remote(s_out, s_in.at[k - 1], s_send.at[k - 1], s_recv.at[k - 1], tensor_at(2 * k))
+        copy.start()
+        s_copies.append(copy)
+
 
     core_copies[3].wait_recv()
     for copy in x_copies:
@@ -292,7 +329,9 @@
     for k in range(n_chip - 1):
         total = total + s_in[k].astype(F32)
     s_all[core] = total.astype(BF16)
-    start(s_copies, s_all.at[core], s_all.at[core], s_send.at[n_chip - 1], s_recv.at[n_chip - 1], other_core)
+    copy = remote(s_all.at[core], s_all.at[core], s_send.at[n_chip - 1], s_recv.at[n_chip - 1], other_core)
+    copy.start()
+    s_copies.append(copy)
 
     for copy in b_copies:
         copy.wait_recv()
@@ -341,7 +380,6 @@
             vmem((2, HALF, width - SHORT), BF16),
             vmem((3, rank, columns), BF16),
             vmem((4, rank, columns), BF16),
-            vmem((rank, columns), BF16),
             vmem((4, rows, columns), F32),
             vmem((4, rows, columns), F32),
             vmem((4, rows, columns), F32),
@@ -359,8 +397,8 @@
             dma((6,)),
             dma((2,)),
             dma((2,)),
-            dma((2 * len(PIECES) + 1,)),
-            dma((2 * len(PIECES) + 1,)),
+            dma((2 * len(PIECES),)),
+            dma((2 * len(PIECES),)),
             dma((2 * len(PIECES),)),
             dma((2 * len(PIECES),)),
             dma((3,)),

time: 39.3 us -> 34.8 us (0.89)
  the two profiles are of different devices: /device:TPU:2 before, /device:TPU:489 now
where the time goes in v5:
time: 34.8 us; the launch traced here: 34.7 us
  Pallas kernels  33.4 us (96%)
  local copies, waits for them, and re-layouts  0.68 us (2%)
  between operations  0.66 us (2%)
    pallas_call x1, Pallas kernels, per_device(): pl.pallas_call(functools.partial(kernel, n_dp, n_tensor), name='adapted_p...  33.4 us

profile of v5, /device:TPU:489, one launch (start us, length us, event | category | flops | bytes accessed | tf_op | source)
XLA Modules:
  0.0 34.7 jit_solution(11076689339710311071)
XLA Ops:
  0.7 33.4 %adapted_projection.1 = bf16[768,128]{1,0:T(8,128)(2,1)S(1)} custom-call(bf16[6,128,1024]{2,1,0:T(8,128)(2,1)} %bitcast.1, bf16[1024,1024]{1,0:T(8,128)(2,1)} %w_hbm.1, bf16[4,64,1024]{2,1,0:T(8,128)(2,1)} %down_hbm.1, bf16[4,64,128]{2,1,0:T(8,128)(2,1)} %up_hbm.1, s32[256]{0:T(256)} %slot_hbm.1, s32[6]{0:T(128)} %ids_hbm.1, s32[1]{0:T(128)S(6)} %copy.10.live_hbm), custom_call_target="tpu_custom_call" | custom-call | flops 2000000000 | bytes 4500000 | tf_op jit(solution)/shard_map/adapted_projection/pallas_call | solution.py:361
  34.1 0.7 %copy.9 = bf16[768,128]{1,0:T(8,128)(2,1)} copy(bf16[768,128]{1,0:T(8,128)(2,1)S(1)} %adapted_projection.1) | data formatting | bytes 393216

commit v6 on v5

--- a/solution.py
+++ b/solution.py
@@ -225,18 +225,25 @@
         for cross in crosses:
             a_copies[2 * (o - 1) + cross].start()
 
-    def serve(o):
-        pick(o)
-        if o == 3:
-            for copy in relay_copies:
-                copy.start()
-        give(o, 0, 1)
-        b_copies[o - 1].start()
-
     def pass_on():
         for there, onward in zip(relay_copies, pass_copies):
             there.wait_recv()
             onward.start()
+
+    def serve(near):
+        late = range(near + 1, 4)
+        for o in late:
+            pick(o)
+            if o < 3:
+                give(o, 0)
+        for copy in relay_copies:
+            copy.start()
+        give(3, 0, 1)
+        for o in reversed(late):
+            if o < 3:
+                give(o, 1)
+        for o in late:
+            b_copies[o - 1].start()
 
     def serve_all():
         pick(1)
@@ -258,13 +265,14 @@
 
     def serve_within(near):
         for o in range(1, 1 + near):
-            serve(o)
+            pick(o)
+            give(o, 0, 1)
+            b_copies[o - 1].start()
         base_send(1)
         base_send(2)
         swap()
         pass_on()
-        for o in range(1 + near, 4):
-            serve(o)
+        serve(near)
 
     def swap():
         for copy in swap_copies:

time: 34.8 us -> 33.4 us (0.960)
  the two profiles are of different devices: /device:TPU:489 before, /device:TPU:233 now
where the time goes in v6:
time: 33.4 us; the launch traced here: 33.2 us
  Pallas kernels  31.9 us (96%)
  local copies, waits for them, and re-layouts  0.68 us (2%)
  between operations  0.66 us (2%)
    pallas_call x1, Pallas kernels, per_device(): pl.pallas_call(functools.partial(kernel, n_dp, n_tensor), name='adapted_p...  31.9 us
    unnamed x1, local copies, waits for them, and re-layouts  0.68 us

profile of v6, /device:TPU:233, one launch (start us, length us, event | category | flops | bytes accessed | tf_op | source)
XLA Modules:
  0.0 33.2 jit_solution(5821388905439362963)
XLA Ops:
  0.7 31.9 %adapted_projection.1 = bf16[768,128]{1,0:T(8,128)(2,1)S(1)} custom-call(bf16[6,128,1024]{2,1,0:T(8,128)(2,1)} %bitcast.1, bf16[1024,1024]{1,0:T(8,128)(2,1)} %w_hbm.1, bf16[4,64,1024]{2,1,0:T(8,128)(2,1)} %down_hbm.1, bf16[4,64,128]{2,1,0:T(8,128)(2,1)} %up_hbm.1, s32[256]{0:T(256)} %slot_hbm.1, s32[6]{0:T(128)} %ids_hbm.1, s32[1]{0:T(128)S(6)} %copy.10.live_hbm), custom_call_target="tpu_custom_call" | custom-call | flops 2000000000 | bytes 4500000 | tf_op jit(solution)/shard_map/adapted_projection/pallas_call | solution.py:369
  32.6 0.7 %copy.9 = bf16[768,128]{1,0:T(8,128)(2,1)} copy(bf16[768,128]{1,0:T(8,128)(2,1)S(1)} %adapted_projection.1) | data formatting | bytes 393216

commit v7 on v6

--- a/solution.py
+++ b/solution.py
@@ -18,6 +18,7 @@
 SHORT = 384
 PIECES = ((384, 256), (640, 384))
 GROUPS = 128 // HALF
+CHUNKS = 3
 STEP = 3
 ORDER = (2, 1, 3, 0)
 
@@ -311,40 +312,47 @@
 
     for copy in swap_copies + a_copies + pass_copies:
         copy.wait_recv()
-    for s in range(segs):
-        o = jnp.minimum(offs[s], 3)
-        part = nt_dot(tok[s], spread(a_in[o, 0])) + nt_dot(tok_other[s], spread(a_in[o, 1]))
-        kept = jnp.where(own_group, part, 0.0)
-        packed = kept[:HALF]
-        for g in range(1, GROUPS):
-            packed = packed + kept[g * HALF : (g + 1) * HALF]
-        s_mine[s] = packed
-        s_out[s] = packed.astype(BF16)
-    for k in range(1, n_chip):
-        copy = remote(s_out, s_in.at[k - 1], s_send.at[k - 1], s_recv.at[k - 1], tensor_at(2 * k))
-        copy.start()
-        s_copies.append(copy)
-
+    chunk = segs // CHUNKS
+    parts = [pl.ds(h * chunk, chunk) for h in range(CHUNKS)]
+    sums = [[] for _ in parts]
+    for h, part in enumerate(parts):
+        for s in range(h * chunk, (h + 1) * chunk):
+            o = jnp.minimum(offs[s], 3)
+            both = nt_dot(tok[s], spread(a_in[o, 0])) + nt_dot(tok_other[s], spread(a_in[o, 1]))
+            kept = jnp.where(own_group, both, 0.0)
+            packed = kept[:HALF]
+            for g in range(1, GROUPS):
+                packed = packed + kept[g * HALF : (g + 1) * HALF]
+            s_mine[s] = packed
+            s_out[s] = packed.astype(BF16)
+        for k in ORDER[:3]:
+            n = h * n_chip + k
+            copy = remote(s_out.at[part], s_in.at[k - 1, part], s_send.at[n], s_recv.at[n], tensor_at(2 * k))
+            copy.start()
+            sums[h].append(copy)
 
     core_copies[3].wait_recv()
     for copy in x_copies:
         copy.wait_recv()
     acc[...] = mine[3] + core_in[3] + x_in[0].astype(F32) + x_in[1].astype(F32) + x_in[2].astype(F32)
 
-    for copy in s_copies:
-        copy.wait_recv()
-    total = s_mine[...]
-    for k in range(n_chip - 1):
-        total = total + s_in[k].astype(F32)
-    s_all[core] = total.astype(BF16)
-    copy = remote(s_all.at[core], s_all.at[core], s_send.at[n_chip - 1], s_recv.at[n_chip - 1], other_core)
-    copy.start()
-    s_copies.append(copy)
+    for h, part in enumerate(parts):
+        for copy in sums[h]:
+            copy.wait_recv()
+        total = s_mine[part]
+        for k in range(n_chip - 1):
+            total = total + s_in[k, part].astype(F32)
+        s_all[core, part] = total.astype(BF16)
+        mine_part = s_all.at[core, part]
+        copy = remote(mine_part, mine_part, s_send.at[h * n_chip], s_recv.at[h * n_chip], other_core)
+        copy.start()
+        s_copies.append(copy)
 
     for copy in b_copies:
         copy.wait_recv()
-    s_copies[-1].wait_recv()
     for s in range(segs):
+        if s % chunk == 0:
+            s_copies[s // chunk].wait_recv()
         factor = b_in[jnp.minimum(offs[s], 3)]
         add = None
         for h in range(2):
@@ -355,7 +363,7 @@
         rows = pl.ds(s * SEG, SEG)
         out_ref[rows, :] = (acc[rows, :] + add).astype(out_ref.dtype)
 
-    for copy in asks + a_copies + swap_copies + relay_copies + pass_copies + b_copies + core_copies + x_copies + s_copies:
+    for copy in asks + a_copies + swap_copies + relay_copies + pass_copies + b_copies + core_copies + x_copies + s_copies + sum(sums, []):
         copy.wait_send()
 
 
@@ -415,8 +423,8 @@
             dma((4,)),
             dma((3,)),
             dma((3,)),
-            dma((chips,)),
-            dma((chips,)),
+            dma((CHUNKS * chips,)),
+            dma((CHUNKS * chips,)),
         ],
         compiler_params=pltpu.CompilerParams(
             collective_id=0, has_side_effects=True, vmem_limit_bytes=63 * 1024 * 1024

time: 33.4 us -> 32.9 us (0.985)
  the two profiles are of different devices: /device:TPU:233 before, /device:TPU:1 now
where the time goes in v7:
time: 32.9 us; the launch traced here: 32.6 us
  Pallas kernels  31.3 us (95%)
  local copies, waits for them, and re-layouts  0.68 us (2%)
  between operations  0.66 us (2%)
    pallas_call x1, Pallas kernels, per_device(): pl.pallas_call(functools.partial(kernel, n_dp, n_tensor), name='adapted_p...  31.3 us
    unnamed x1, local copies, waits for them, and re-layouts  0.68 us

profile of v7, /device:TPU:1, one launch (start us, length us, event | category | flops | bytes accessed | tf_op | source)
XLA Modules:
  0.0 32.6 jit_solution(9226752827469046280)
XLA Ops:
  0.7 31.3 %adapted_projection.1 = bf16[768,128]{1,0:T(8,128)(2,1)S(1)} custom-call(bf16[6,128,1024]{2,1,0:T(8,128)(2,1)} %bitcast.1, bf16[1024,1024]{1,0:T(8,128)(2,1)} %w_hbm.1, bf16[4,64,1024]{2,1,0:T(8,128)(2,1)} %down_hbm.1, bf16[4,64,128]{2,1,0:T(8,128)(2,1)} %up_hbm.1, s32[256]{0:T(256)} %slot_hbm.1, s32[6]{0:T(128)} %ids_hbm.1, s32[1]{0:T(128)S(6)} %copy.10.live_hbm), custom_call_target="tpu_custom_call" | custom-call | flops 2000000000 | bytes 4500000 | tf_op jit(solution)/shard_map/adapted_projection/pallas_call | solution.py:377
  32.0 0.7 %copy.9 = bf16[768,128]{1,0:T(8,128)(2,1)} copy(bf16[768,128]{1,0:T(8,128)(2,1)S(1)} %adapted_projection.1) | data formatting | bytes 393216

commit v8 on v7

--- a/solution.py
+++ b/solution.py
@@ -249,6 +249,7 @@
     def serve_all():
         pick(1)
         give(1, 0)
+        base_send(0)
         pick(2)
         give(2, 0)
         pick(3)
@@ -265,6 +266,7 @@
         pass_on()
 
     def serve_within(near):
+        base_send(0)
         for o in range(1, 1 + near):
             pick(o)
             give(o, 0, 1)
@@ -289,7 +291,6 @@
     b_in[0] = up[wanted[0]]
     base_block(2)
     base_block(3)
-    base_send(0)
     swap_copies.append(remote(tok, tok_other, swap_send.at[0], swap_recv.at[0], other_core))
     swap_copies.append(remote(a_out.at[0, rank_half(1)], a_in.at[0, 1], swap_send.at[1], swap_recv.at[1], other_core))
 

time: 32.9 us -> 33.2 us (level)
  the two profiles are of different devices: /device:TPU:1 before, /device:TPU:249 now
where the time goes in v8:
time: 33.2 us; the launch traced here: 33.1 us
  Pallas kernels  31.8 us (96%)
  local copies, waits for them, and re-layouts  0.68 us (2%)
  between operations  0.66 us (2%)
    pallas_call x1, Pallas kernels, per_device(): pl.pallas_call(functools.partial(kernel, n_dp, n_tensor), name='adapted_p...  31.8 us
    unnamed x1, local copies, waits for them, and re-layouts  0.68 us

profile of v8, /device:TPU:249, one launch (start us, length us, event | category | flops | bytes accessed | tf_op | source)
XLA Modules:
  0.0 33.1 jit_solution(15141907326175280936)
XLA Ops:
  0.7 31.8 %adapted_projection.1 = bf16[768,128]{1,0:T(8,128)(2,1)S(1)} custom-call(bf16[6,128,1024]{2,1,0:T(8,128)(2,1)} %bitcast.1, bf16[1024,1024]{1,0:T(8,128)(2,1)} %w_hbm.1, bf16[4,64,1024]{2,1,0:T(8,128)(2,1)} %down_hbm.1, bf16[4,64,128]{2,1,0:T(8,128)(2,1)} %up_hbm.1, s32[256]{0:T(256)} %slot_hbm.1, s32[6]{0:T(128)} %ids_hbm.1, s32[1]{0:T(128)S(6)} %copy.10.live_hbm), custom_call_target="tpu_custom_call" | custom-call | flops 2000000000 | bytes 4500000 | tf_op jit(solution)/shard_map/adapted_projection/pallas_call | solution.py:378
  32.4 0.7 %copy.9 = bf16[768,128]{1,0:T(8,128)(2,1)} copy(bf16[768,128]{1,0:T(8,128)(2,1)S(1)} %adapted_projection.1) | data formatting | bytes 393216
